TPU v7x, 256 devices: a whole 4x4x8 slice. The times are simulated.
256 devices in a mesh: dp: 16 (over z_hi, x), ctx: 16 (over y, z_lo, core).
Axes of the slice: x: 4, y: 4, z: 8 (z_hi: 4, z_lo: 2; z = z_hi * 2 + z_lo), core: 2. Of those that a mesh axis runs over, the one named last changes fastest.
Arguments:
- doc_lengths: int32 [64], replicated, may hold values from 1 to 1792, 65536 in all
- queries: bfloat16 [65536, 1024], P(('dp', 'ctx')), may hold values from -6 to 6
- key_rows: bfloat16 [65536, 128], P(('dp', 'ctx')), may hold values from -6 to 6
- value_rows: bfloat16 [65536, 128], P(('dp', 'ctx')), may hold values from -6 to 6
- grad_out: bfloat16 [65536, 1024], P(('dp', 'ctx')), may hold values from -6 to 6
Outputs:
- attn_out: bfloat16 [65536, 1024], P(('dp', 'ctx'))
- grad_queries: bfloat16 [65536, 1024], P(('dp', 'ctx'))
- grad_keys: bfloat16 [65536, 128], P(('dp', 'ctx'))
- grad_values: bfloat16 [65536, 128], P(('dp', 'ctx'))
Inputs may be any that keep to these rules, and one draw needn't show every extreme that they name: `doc_lengths`: the lengths sum to 65536; each is at most 1792, and one document has exactly 1792 tokens.
All inputs are finite; a program needn't handle non-finite values.
Results may differ from a plain program's by a relative error of at most 0.034.
Values may be sent and summed in bfloat16 or wider, within the bound.
No kernel may reach another device: no remote copies, remote signals or barrier semaphores. Data moves between devices by JAX's collectives and lax.ppermute only.
A program may use at most 64 MiB of HBM per device.

v0:
```python
import math

import jax
import jax.numpy as jnp
from jax import lax
from jax.sharding import PartitionSpec as P

REACH = 8


def shifted(value, axis, steps):
    count = lax.axis_size(axis)
    first, last = (max(0, -steps), min(count, count - steps))
    return lax.ppermute(value, axis, [(source, source + steps) for source in range(first, last)])


def attend_block(
    q_block, win_keys, win_values, g_block, q_pos, key_pos, q_begin, head_count, head_size
):
    tokens_here = q_block.shape[0]
    span_len = win_keys.shape[0]
    scale = head_size ** (-0.5)
    query_rows = q_block.reshape(tokens_here * head_count, head_size)
    grad_rows = g_block.reshape(tokens_here * head_count, head_size)
    scores = jnp.dot(query_rows, win_keys.T, preferred_element_type=jnp.float32) * scale
    scores = scores.reshape(tokens_here, head_count, span_len)
    allowed = (key_pos[None, :] <= q_pos[:, None]) & (key_pos[None, :] >= q_begin[:, None])
    scores = jnp.where(allowed[:, None, :], scores, -jnp.inf)
    row_max = jnp.max(scores, axis=2, keepdims=True)
    weights = jnp.exp(scores - row_max)
    row_sum = jnp.sum(weights, axis=2, keepdims=True)
    weights_bf = weights.astype(jnp.bfloat16).reshape(tokens_here * head_count, span_len)
    out_rows = (
        jnp.dot(weights_bf, win_values, preferred_element_type=jnp.float32) / row_sum.reshape(-1, 1)
    ).astype(jnp.bfloat16)
    row_dot = jnp.sum(grad_rows.astype(jnp.float32) * out_rows.astype(jnp.float32), axis=1)
    probs = (weights / row_sum).reshape(tokens_here * head_count, span_len)
    probs_bf = probs.astype(jnp.bfloat16)
    grad_probs = jnp.dot(grad_rows, win_values.T, preferred_element_type=jnp.float32)
    grad_scores = (probs * (grad_probs - row_dot[:, None])).astype(jnp.bfloat16)
    grad_query = (
        jnp.dot(grad_scores, win_keys, preferred_element_type=jnp.float32) * scale
    ).astype(jnp.bfloat16)
    grad_key = jnp.dot(grad_scores.T, query_rows, preferred_element_type=jnp.float32) * scale
    grad_value = jnp.dot(probs_bf.T, grad_rows, preferred_element_type=jnp.float32)
    return (
        out_rows.reshape(tokens_here, head_count * head_size),
        grad_query.reshape(tokens_here, head_count * head_size),
        grad_key,
        grad_value,
    )


def local(doc_lengths, queries, key_rows, value_rows, grad_out):
    rows_dev = queries.shape[0]
    head_size = key_rows.shape[1]
    head_count = queries.shape[1] // head_size
    window = REACH * rows_dev
    margin = (REACH - 1) * rows_dev
    dev_rank = lax.axis_index(("dp", "ctx"))
    first_row = dev_rank * rows_dev
    doc_starts = jnp.cumsum(doc_lengths) - doc_lengths
    tok_index = first_row + jnp.arange(rows_dev, dtype=jnp.int32)
    key_index = first_row - margin + jnp.arange(window, dtype=jnp.int32)
    doc_begin = jnp.max(
        jnp.where(doc_starts[None, :] <= tok_index[:, None], doc_starts[None, :], 0), axis=1
    )
    key_parts = [key_rows]
    value_parts = [value_rows]
    for distance in range(1, REACH):
        received = shifted((key_rows, value_rows), ("dp", "ctx"), distance)
        key_parts.insert(0, received[0])
        value_parts.insert(0, received[1])
    win_keys = jnp.concatenate(key_parts, axis=0)
    win_values = jnp.concatenate(value_parts, axis=0)
    block_rows = math.gcd(64, rows_dev)
    block_count = rows_dev // block_rows
    q_blocks = queries.reshape(block_count, block_rows, queries.shape[1])
    g_blocks = grad_out.reshape(block_count, block_rows, grad_out.shape[1])
    pos_blocks = tok_index.reshape(block_count, block_rows)
    begin_blocks = doc_begin.reshape(block_count, block_rows)

    def fold_step(totals, item):
        q_block, g_block, q_pos, q_begin = item
        out_rows, grad_query, grad_key, grad_value = attend_block(
            q_block, win_keys, win_values, g_block, q_pos, key_index, q_begin, head_count, head_size
        )
        return ((totals[0] + grad_key, totals[1] + grad_value), (out_rows, grad_query))

    empty = jnp.zeros((window, head_size), jnp.float32)
    totals, stacked = lax.scan(
        fold_step, (empty, empty), (q_blocks, g_blocks, pos_blocks, begin_blocks)
    )
    attn_out = stacked[0].reshape(rows_dev, queries.shape[1])
    grad_queries = stacked[1].reshape(rows_dev, queries.shape[1])
    win_grad_keys, win_grad_values = totals
    own_keys = win_grad_keys[margin:]
    own_values = win_grad_values[margin:]
    remote_keys = (
        win_grad_keys[:margin].astype(jnp.bfloat16).reshape(REACH - 1, rows_dev, head_size)
    )
    remote_values = (
        win_grad_values[:margin].astype(jnp.bfloat16).reshape(REACH - 1, rows_dev, head_size)
    )
    sum_keys = own_keys
    sum_values = own_values
    for distance in range(1, REACH):
        slot = REACH - 1 - distance
        received = shifted((remote_keys[slot], remote_values[slot]), ("dp", "ctx"), -distance)
        sum_keys = sum_keys + received[0].astype(jnp.float32)
        sum_values = sum_values + received[1].astype(jnp.float32)
    return (attn_out, grad_queries, sum_keys.astype(jnp.bfloat16), sum_values.astype(jnp.bfloat16))


def solution(mesh):
    return jax.shard_map(
        local,
        mesh=mesh,
        in_specs=(
            P(),
            P(("dp", "ctx"), None),
            P(("dp", "ctx"), None),
            P(("dp", "ctx"), None),
            P(("dp", "ctx"), None),
        ),
        out_specs=(
            P(("dp", "ctx"), None),
            P(("dp", "ctx"), None),
            P(("dp", "ctx"), None),
            P(("dp", "ctx"), None),
        ),
        check_vma=False,
    )
```

profile of v0, /device:TPU:167, one launch (start us, length us, event | category | flops | bytes accessed | tf_op | source)
XLA Modules:
  0.0 246.5 jit_solution(4045934599992571980)
XLA Ops:
  0.6 3.7 %collective-permute-start.5 = (bf16[256,128]{1,0:T(8,128)(2,1)}, bf16[256,128]{1,0:T(8,128)(2,1)S(1)}, u32[]{:S(2)}, u32[]{:S(2)}) collective-permute-start(bf16[256,128]{1,0:T(8,128)(2,1)} %param.9), channel_id=1, source_target_pairs={{0,2},{1,3},{2,4},{3,5},{4,6},{5,7},{6,8},{7,9},{8,10},{9,11},{10,... | collective-permute-start | bytes 196616 | tf_op jit(solution)/shard_map/ppermute | solution.py:14
  4.3 4.0 %collective-permute-start.4 = (bf16[256,128]{1,0:T(8,128)(2,1)}, bf16[256,128]{1,0:T(8,128)(2,1)S(1)}, u32[]{:S(2)}, u32[]{:S(2)}) collective-permute-start(bf16[256,128]{1,0:T(8,128)(2,1)} %param.9), channel_id=1, source_target_pairs={{0,3},{1,4},{2,5},{3,6},{4,7},{5,8},{6,9},{7,10},{8,11},{9,12},{10... | collective-permute-start | bytes 196616 | tf_op jit(solution)/shard_map/ppermute | solution.py:14
  8.3 2.9 %collective-permute-start.3 = (bf16[256,128]{1,0:T(8,128)(2,1)}, bf16[256,128]{1,0:T(8,128)(2,1)S(1)}, u32[]{:S(2)}, u32[]{:S(2)}) collective-permute-start(bf16[256,128]{1,0:T(8,128)(2,1)} %param.9), channel_id=1, source_target_pairs={{0,4},{1,5},{2,6},{3,7},{4,8},{5,9},{6,10},{7,11},{8,12},{9,13},{1... | collective-permute-start | bytes 196616 | tf_op jit(solution)/shard_map/ppermute | solution.py:14
  11.3 3.3 %collective-permute-start.2 = (bf16[256,128]{1,0:T(8,128)(2,1)}, bf16[256,128]{1,0:T(8,128)(2,1)S(1)}, u32[]{:S(2)}, u32[]{:S(2)}) collective-permute-start(bf16[256,128]{1,0:T(8,128)(2,1)} %param.9), channel_id=1, source_target_pairs={{0,5},{1,6},{2,7},{3,8},{4,9},{5,10},{6,11},{7,12},{8,13},{9,14},{... | collective-permute-start | bytes 196616 | tf_op jit(solution)/shard_map/ppermute | solution.py:14
  14.5 4.5 %collective-permute-start.7 = (bf16[256,128]{1,0:T(8,128)(2,1)}, bf16[256,128]{1,0:T(8,128)(2,1)S(1)}, u32[]{:S(2)}, u32[]{:S(2)}) collective-permute-start(bf16[256,128]{1,0:T(8,128)(2,1)} %param.10), channel_id=1, source_target_pairs={{0,7},{1,8},{2,9},{3,10},{4,11},{5,12},{6,13},{7,14},{8,15},{9,16}... | collective-permute-start | bytes 196616 | tf_op jit(solution)/shard_map/ppermute | solution.py:14
  20.9 2.4 collective-permute-done.7
  23.3 3.7 %collective-permute-start.8 = (bf16[256,128]{1,0:T(8,128)(2,1)}, bf16[256,128]{1,0:T(8,128)(2,1)S(1)}, u32[]{:S(2)}, u32[]{:S(2)}) collective-permute-start(bf16[256,128]{1,0:T(8,128)(2,1)} %param.10), channel_id=1, source_target_pairs={{0,6},{1,7},{2,8},{3,9},{4,10},{5,11},{6,12},{7,13},{8,14},{9,15},... | collective-permute-start | bytes 196616 | tf_op jit(solution)/shard_map/ppermute | solution.py:14
  27.0 4.5 %collective-permute-done.8 = bf16[256,128]{1,0:T(8,128)(2,1)S(1)} collective-permute-done((bf16[256,128]{1,0:T(8,128)(2,1)}, bf16[256,128]{1,0:T(8,128)(2,1)S(1)}, u32[]{:S(2)}, u32[]{:S(2)}) %collective-permute-start.8) | collective-permute-done | bytes 65568 | tf_op jit(solution)/shard_map/ppermute | solution.py:14
  31.6 3.1 %collective-permute-start.9 = (bf16[256,128]{1,0:T(8,128)(2,1)}, bf16[256,128]{1,0:T(8,128)(2,1)S(1)}, u32[]{:S(2)}, u32[]{:S(2)}) collective-permute-start(bf16[256,128]{1,0:T(8,128)(2,1)} %param.10), channel_id=1, source_target_pairs={{0,5},{1,6},{2,7},{3,8},{4,9},{5,10},{6,11},{7,12},{8,13},{9,14},{... | collective-permute-start | bytes 196616 | tf_op jit(solution)/shard_map/ppermute | solution.py:14
  34.7 5.3 %collective-permute-done.9 = bf16[256,128]{1,0:T(8,128)(2,1)S(1)} collective-permute-done((bf16[256,128]{1,0:T(8,128)(2,1)}, bf16[256,128]{1,0:T(8,128)(2,1)S(1)}, u32[]{:S(2)}, u32[]{:S(2)}) %collective-permute-start.9) | collective-permute-done | bytes 65568 | tf_op jit(solution)/shard_map/ppermute | solution.py:14
  40.0 1.9 collective-permute-start.10
  41.9 5.9 %collective-permute-done.10 = bf16[256,128]{1,0:T(8,128)(2,1)S(1)} collective-permute-done((bf16[256,128]{1,0:T(8,128)(2,1)}, bf16[256,128]{1,0:T(8,128)(2,1)S(1)}, u32[]{:S(2)}, u32[]{:S(2)}) %collective-permute-start.10) | collective-permute-done | bytes 65568 | tf_op jit(solution)/shard_map/ppermute | solution.py:14
  47.9 1.9 collective-permute-start.11
  49.8 4.4 %collective-permute-done.11 = bf16[256,128]{1,0:T(8,128)(2,1)S(1)} collective-permute-done((bf16[256,128]{1,0:T(8,128)(2,1)}, bf16[256,128]{1,0:T(8,128)(2,1)S(1)}, u32[]{:S(2)}, u32[]{:S(2)}) %collective-permute-start.11) | collective-permute-done | bytes 65568 | tf_op jit(solution)/shard_map/ppermute | solution.py:14
  54.2 2.7 %collective-permute-start.12 = (bf16[256,128]{1,0:T(8,128)(2,1)}, bf16[256,128]{1,0:T(8,128)(2,1)S(1)}, u32[]{:S(2)}, u32[]{:S(2)}) collective-permute-start(bf16[256,128]{1,0:T(8,128)(2,1)} %param.10), channel_id=1, source_target_pairs={{0,2},{1,3},{2,4},{3,5},{4,6},{5,7},{6,8},{7,9},{8,10},{9,11},{10,... | collective-permute-start | bytes 196616 | tf_op jit(solution)/shard_map/ppermute | solution.py:14
  56.9 3.6 %collective-permute-done.12 = bf16[256,128]{1,0:T(8,128)(2,1)S(1)} collective-permute-done((bf16[256,128]{1,0:T(8,128)(2,1)}, bf16[256,128]{1,0:T(8,128)(2,1)S(1)}, u32[]{:S(2)}, u32[]{:S(2)}) %collective-permute-start.12) | collective-permute-done | bytes 65568 | tf_op jit(solution)/shard_map/ppermute | solution.py:14
  60.5 4.8 %collective-permute-start.13 = (bf16[256,128]{1,0:T(8,128)(2,1)}, bf16[256,128]{1,0:T(8,128)(2,1)S(1)}, u32[]{:S(2)}, u32[]{:S(2)}) collective-permute-start(bf16[256,128]{1,0:T(8,128)(2,1)} %param.10), channel_id=1, source_target_pairs={{0,1},{1,2},{2,3},{3,4},{4,5},{5,6},{6,7},{7,8},{8,9},{9,10},{10,1... | collective-permute-start | bytes 196616 | tf_op jit(solution)/shard_map/ppermute | solution.py:14
  65.4 1.6 collective-permute-done.13
  67.0 9.3 %collective-permute-start = (bf16[256,128]{1,0:T(8,128)(2,1)}, bf16[256,128]{1,0:T(8,128)(2,1)S(1)}, u32[]{:S(2)}, u32[]{:S(2)}) collective-permute-start(bf16[256,128]{1,0:T(8,128)(2,1)} %param.9), channel_id=1, source_target_pairs={{0,7},{1,8},{2,9},{3,10},{4,11},{5,12},{6,13},{7,14},{8,15},{9,16}... | collective-permute-start | bytes 196616 | tf_op jit(solution)/shard_map/ppermute | solution.py:14
  77.9 22.0 %collective-permute-start.1 = (bf16[256,128]{1,0:T(8,128)(2,1)}, bf16[256,128]{1,0:T(8,128)(2,1)S(1)}, u32[]{:S(2)}, u32[]{:S(2)}) collective-permute-start(bf16[256,128]{1,0:T(8,128)(2,1)} %param.9), channel_id=1, source_target_pairs={{0,6},{1,7},{2,8},{3,9},{4,10},{5,11},{6,12},{7,13},{8,14},{9,15},... | collective-permute-start | bytes 196616 | tf_op jit(solution)/shard_map/ppermute | solution.py:14
  100.0 1.6 collective-permute-done.1
  101.6 1.9 collective-permute-start.6
  103.6 1.5 collective-permute-done.6
  106.0 61.2 %while.17 = (s32[]{:T(128)}, f32[2048,128]{1,0:T(8,128)S(1)}, f32[2048,128]{1,0:T(8,128)S(1)}, bf16[4,64,1024]{2,1,0:T(8,128)(2,1)}, bf16[4,64,1024]{2,1,0:T(8,1...) while((s32[]{:T(128)}, f32[2048,128]{1,0:T(8,128)S(1)}, ...), condition=%wide.region_6.7_spmd.clone, body=%wide.region_2.6_spmd.clone.sunk | while | flops 1636958720 | bytes 75669272 | solution.py:91
  112.4 4.2 %convolution_add_fusion.2 = f32[2048,128]{1,0:T(8,128)S(1)} fusion(bf16[512,128]{1,0:T(8,128)(2,1)S(1)} %reshape.187, f32[2048,128]{1,0:T(8,128)S(1)} %get-tuple-element.260, pred[]{:T(512)S(6)} %compare.3, f32[512,2048]{1,0:T(8,128)} %copy-done, f32[512]{0:T(512)S(1)} %fusion.66, f32[512]{0:T(512)S(1)} %get-tuple-element.239, ...), kind=kOutput, calls=%fused_computation.5.clone.1 | convolution fusion | flops 274202624 | bytes 6557697 | tf_op jit(solution)/shard_map/while/body/eval_jaxpr/dot_general | solution.py:45
  116.6 2.0 multiply_convert_fusion.2
  126.0 1.4 multiply_reduce_fusion.2
  127.7 4.2 %convolution_add_fusion.2 = f32[2048,128]{1,0:T(8,128)S(1)} fusion(bf16[512,128]{1,0:T(8,128)(2,1)S(1)} %reshape.187, f32[2048,128]{1,0:T(8,128)S(1)} %get-tuple-element.260, pred[]{:T(512)S(6)} %compare.3, f32[512,2048]{1,0:T(8,128)} %copy-done, f32[512]{0:T(512)S(1)} %fusion.66, f32[512]{0:T(512)S(1)} %get-tuple-element.239, ...), kind=kOutput, calls=%fused_computation.5.clone.1 | convolution fusion | flops 274202624 | bytes 6557697 | tf_op jit(solution)/shard_map/while/body/eval_jaxpr/dot_general | solution.py:45
  131.9 2.0 multiply_convert_fusion.2
  143.0 4.2 %convolution_add_fusion.2 = f32[2048,128]{1,0:T(8,128)S(1)} fusion(bf16[512,128]{1,0:T(8,128)(2,1)S(1)} %reshape.187, f32[2048,128]{1,0:T(8,128)S(1)} %get-tuple-element.260, pred[]{:T(512)S(6)} %compare.3, f32[512,2048]{1,0:T(8,128)} %copy-done, f32[512]{0:T(512)S(1)} %fusion.66, f32[512]{0:T(512)S(1)} %get-tuple-element.239, ...), kind=kOutput, calls=%fused_computation.5.clone.1 | convolution fusion | flops 274202624 | bytes 6557697 | tf_op jit(solution)/shard_map/while/body/eval_jaxpr/dot_general | solution.py:45
  147.2 2.0 multiply_convert_fusion.2
  158.2 4.2 %convolution_add_fusion.2 = f32[2048,128]{1,0:T(8,128)S(1)} fusion(bf16[512,128]{1,0:T(8,128)(2,1)S(1)} %reshape.187, f32[2048,128]{1,0:T(8,128)S(1)} %get-tuple-element.260, pred[]{:T(512)S(6)} %compare.3, f32[512,2048]{1,0:T(8,128)} %copy-done, f32[512]{0:T(512)S(1)} %fusion.66, f32[512]{0:T(512)S(1)} %get-tuple-element.239, ...), kind=kOutput, calls=%fused_computation.5.clone.1 | convolution fusion | flops 274202624 | bytes 6557697 | tf_op jit(solution)/shard_map/while/body/eval_jaxpr/dot_general | solution.py:45
  162.5 2.0 multiply_convert_fusion.2
  167.3 1.9 collective-permute-start.14
  169.2 1.9 collective-permute-start.20
  171.1 1.9 collective-permute-start.19
  173.1 4.6 %collective-permute-start.18 = (bf16[256,128]{1,0:T(8,128)(2,1)S(1)}, bf16[256,128]{1,0:T(8,128)(2,1)S(1)}, u32[]{:S(2)}, u32[]{:S(2)}) collective-permute-start(bf16[256,128]{1,0:T(8,128)(2,1)S(1)} %get-tuple-element.155), channel_id=1, source_target_pairs={{5,0},{6,1},{7,2},{8,3},{9,4},{10,5},{11,6},{12,7},{13,8},{14,9},{... | collective-permute-start | bytes 196616 | tf_op jit(solution)/shard_map/ppermute | solution.py:14
  177.7 1.9 collective-permute-start.17
  179.8 3.7 %collective-permute-start.16 = (bf16[256,128]{1,0:T(8,128)(2,1)S(1)}, bf16[256,128]{1,0:T(8,128)(2,1)S(1)}, u32[]{:S(2)}, u32[]{:S(2)}) collective-permute-start(bf16[256,128]{1,0:T(8,128)(2,1)S(1)} %get-tuple-element.157), channel_id=1, source_target_pairs={{3,0},{4,1},{5,2},{6,3},{7,4},{8,5},{9,6},{10,7},{11,8},{12,9},{13... | collective-permute-start | bytes 196616 | tf_op jit(solution)/shard_map/ppermute | solution.py:14
  183.6 1.9 collective-permute-start.15
  185.6 2.2 collective-permute-start.21
  187.7 15.3 %collective-permute-start.27 = (bf16[256,128]{1,0:T(8,128)(2,1)S(1)}, bf16[256,128]{1,0:T(8,128)(2,1)S(1)}, u32[]{:S(2)}, u32[]{:S(2)}) collective-permute-start(bf16[256,128]{1,0:T(8,128)(2,1)S(1)} %get-tuple-element.146), channel_id=1, source_target_pairs={{7,0},{8,1},{9,2},{10,3},{11,4},{12,5},{13,6},{14,7},{15,8},{16,9}... | collective-permute-start | bytes 196616 | tf_op jit(solution)/shard_map/ppermute | solution.py:14
  203.0 9.6 %collective-permute-start.26 = (bf16[256,128]{1,0:T(8,128)(2,1)S(1)}, bf16[256,128]{1,0:T(8,128)(2,1)S(1)}, u32[]{:S(2)}, u32[]{:S(2)}) collective-permute-start(bf16[256,128]{1,0:T(8,128)(2,1)S(1)} %get-tuple-element.147), channel_id=1, source_target_pairs={{6,0},{7,1},{8,2},{9,3},{10,4},{11,5},{12,6},{13,7},{14,8},{15,9},... | collective-permute-start | bytes 196616 | tf_op jit(solution)/shard_map/ppermute | solution.py:14
  212.6 7.7 %collective-permute-start.25 = (bf16[256,128]{1,0:T(8,128)(2,1)S(1)}, bf16[256,128]{1,0:T(8,128)(2,1)S(1)}, u32[]{:S(2)}, u32[]{:S(2)}) collective-permute-start(bf16[256,128]{1,0:T(8,128)(2,1)S(1)} %get-tuple-element.148), channel_id=1, source_target_pairs={{5,0},{6,1},{7,2},{8,3},{9,4},{10,5},{11,6},{12,7},{13,8},{14,9},{... | collective-permute-start | bytes 196616 | tf_op jit(solution)/shard_map/ppermute | solution.py:14
  220.3 12.4 %collective-permute-start.24 = (bf16[256,128]{1,0:T(8,128)(2,1)S(1)}, bf16[256,128]{1,0:T(8,128)(2,1)S(1)}, u32[]{:S(2)}, u32[]{:S(2)}) collective-permute-start(bf16[256,128]{1,0:T(8,128)(2,1)S(1)} %get-tuple-element.149), channel_id=1, source_target_pairs={{4,0},{5,1},{6,2},{7,3},{8,4},{9,5},{10,6},{11,7},{12,8},{13,9},{1... | collective-permute-start | bytes 196616 | tf_op jit(solution)/shard_map/ppermute | solution.py:14
  232.7 6.2 %collective-permute-start.23 = (bf16[256,128]{1,0:T(8,128)(2,1)S(1)}, bf16[256,128]{1,0:T(8,128)(2,1)S(1)}, u32[]{:S(2)}, u32[]{:S(2)}) collective-permute-start(bf16[256,128]{1,0:T(8,128)(2,1)S(1)} %get-tuple-element.150), channel_id=1, source_target_pairs={{3,0},{4,1},{5,2},{6,3},{7,4},{8,5},{9,6},{10,7},{11,8},{12,9},{13... | collective-permute-start | bytes 196616 | tf_op jit(solution)/shard_map/ppermute | solution.py:14
  238.9 2.2 collective-permute-start.22
  241.9 3.9 %collective-permute-done.22 = bf16[256,128]{1,0:T(8,128)(2,1)S(1)} collective-permute-done((bf16[256,128]{1,0:T(8,128)(2,1)S(1)}, bf16[256,128]{1,0:T(8,128)(2,1)S(1)}, u32[]{:S(2)}, u32[]{:S(2)}) %collective-permute-start.22) | collective-permute-done | bytes 65568 | tf_op jit(solution)/shard_map/ppermute | solution.py:14
  (157 shorter events, 40.4 us)
Async XLA Ops:
  0.6 103.0 %collective-permute-start.5 = (bf16[256,128]{1,0:T(8,128)(2,1)}, bf16[256,128]{1,0:T(8,128)(2,1)S(1)}, u32[]{:S(2)}, u32[]{:S(2)}) collective-permute-start(bf16[256,128]{1,0:T(8,128)(2,1)} %param.9), channel_id=1, source_target_pairs={{0,2},{1,3},{2,4},{3,5},{4,6},{5,7},{6,8},{7,9},{8,10},{9,11},{10,... | collective-permute-start | bytes 196616 | tf_op jit(solution)/shard_map/ppermute | solution.py:14
  4.3 99.3 %collective-permute-start.4 = (bf16[256,128]{1,0:T(8,128)(2,1)}, bf16[256,128]{1,0:T(8,128)(2,1)S(1)}, u32[]{:S(2)}, u32[]{:S(2)}) collective-permute-start(bf16[256,128]{1,0:T(8,128)(2,1)} %param.9), channel_id=1, source_target_pairs={{0,3},{1,4},{2,5},{3,6},{4,7},{5,8},{6,9},{7,10},{8,11},{9,12},{10... | collective-permute-start | bytes 196616 | tf_op jit(solution)/shard_map/ppermute | solution.py:14
  8.3 95.2 %collective-permute-start.3 = (bf16[256,128]{1,0:T(8,128)(2,1)}, bf16[256,128]{1,0:T(8,128)(2,1)S(1)}, u32[]{:S(2)}, u32[]{:S(2)}) collective-permute-start(bf16[256,128]{1,0:T(8,128)(2,1)} %param.9), channel_id=1, source_target_pairs={{0,4},{1,5},{2,6},{3,7},{4,8},{5,9},{6,10},{7,11},{8,12},{9,13},{1... | collective-permute-start | bytes 196616 | tf_op jit(solution)/shard_map/ppermute | solution.py:14
  11.3 92.2 %collective-permute-start.2 = (bf16[256,128]{1,0:T(8,128)(2,1)}, bf16[256,128]{1,0:T(8,128)(2,1)S(1)}, u32[]{:S(2)}, u32[]{:S(2)}) collective-permute-start(bf16[256,128]{1,0:T(8,128)(2,1)} %param.9), channel_id=1, source_target_pairs={{0,5},{1,6},{2,7},{3,8},{4,9},{5,10},{6,11},{7,12},{8,13},{9,14},{... | collective-permute-start | bytes 196616 | tf_op jit(solution)/shard_map/ppermute | solution.py:14
  14.5 8.8 %collective-permute-start.7 = (bf16[256,128]{1,0:T(8,128)(2,1)}, bf16[256,128]{1,0:T(8,128)(2,1)S(1)}, u32[]{:S(2)}, u32[]{:S(2)}) collective-permute-start(bf16[256,128]{1,0:T(8,128)(2,1)} %param.10), channel_id=1, source_target_pairs={{0,7},{1,8},{2,9},{3,10},{4,11},{5,12},{6,13},{7,14},{8,15},{9,16}... | collective-permute-start | bytes 196616 | tf_op jit(solution)/shard_map/ppermute | solution.py:14
  23.3 8.2 %collective-permute-start.8 = (bf16[256,128]{1,0:T(8,128)(2,1)}, bf16[256,128]{1,0:T(8,128)(2,1)S(1)}, u32[]{:S(2)}, u32[]{:S(2)}) collective-permute-start(bf16[256,128]{1,0:T(8,128)(2,1)} %param.10), channel_id=1, source_target_pairs={{0,6},{1,7},{2,8},{3,9},{4,10},{5,11},{6,12},{7,13},{8,14},{9,15},... | collective-permute-start | bytes 196616 | tf_op jit(solution)/shard_map/ppermute | solution.py:14
  31.6 8.4 %collective-permute-start.9 = (bf16[256,128]{1,0:T(8,128)(2,1)}, bf16[256,128]{1,0:T(8,128)(2,1)S(1)}, u32[]{:S(2)}, u32[]{:S(2)}) collective-permute-start(bf16[256,128]{1,0:T(8,128)(2,1)} %param.10), channel_id=1, source_target_pairs={{0,5},{1,6},{2,7},{3,8},{4,9},{5,10},{6,11},{7,12},{8,13},{9,14},{... | collective-permute-start | bytes 196616 | tf_op jit(solution)/shard_map/ppermute | solution.py:14
  40.0 7.9 %collective-permute-start.10 = (bf16[256,128]{1,0:T(8,128)(2,1)}, bf16[256,128]{1,0:T(8,128)(2,1)S(1)}, u32[]{:S(2)}, u32[]{:S(2)}) collective-permute-start(bf16[256,128]{1,0:T(8,128)(2,1)} %param.10), channel_id=1, source_target_pairs={{0,4},{1,5},{2,6},{3,7},{4,8},{5,9},{6,10},{7,11},{8,12},{9,13},{1... | collective-permute-start | bytes 196616 | tf_op jit(solution)/shard_map/ppermute | solution.py:14
  47.9 6.3 %collective-permute-start.11 = (bf16[256,128]{1,0:T(8,128)(2,1)}, bf16[256,128]{1,0:T(8,128)(2,1)S(1)}, u32[]{:S(2)}, u32[]{:S(2)}) collective-permute-start(bf16[256,128]{1,0:T(8,128)(2,1)} %param.10), channel_id=1, source_target_pairs={{0,3},{1,4},{2,5},{3,6},{4,7},{5,8},{6,9},{7,10},{8,11},{9,12},{10... | collective-permute-start | bytes 196616 | tf_op jit(solution)/shard_map/ppermute | solution.py:14
  54.2 6.4 %collective-permute-start.12 = (bf16[256,128]{1,0:T(8,128)(2,1)}, bf16[256,128]{1,0:T(8,128)(2,1)S(1)}, u32[]{:S(2)}, u32[]{:S(2)}) collective-permute-start(bf16[256,128]{1,0:T(8,128)(2,1)} %param.10), channel_id=1, source_target_pairs={{0,2},{1,3},{2,4},{3,5},{4,6},{5,7},{6,8},{7,9},{8,10},{9,11},{10,... | collective-permute-start | bytes 196616 | tf_op jit(solution)/shard_map/ppermute | solution.py:14
  60.5 6.4 %collective-permute-start.13 = (bf16[256,128]{1,0:T(8,128)(2,1)}, bf16[256,128]{1,0:T(8,128)(2,1)S(1)}, u32[]{:S(2)}, u32[]{:S(2)}) collective-permute-start(bf16[256,128]{1,0:T(8,128)(2,1)} %param.10), channel_id=1, source_target_pairs={{0,1},{1,2},{2,3},{3,4},{4,5},{5,6},{6,7},{7,8},{8,9},{9,10},{10,1... | collective-permute-start | bytes 196616 | tf_op jit(solution)/shard_map/ppermute | solution.py:14
  67.0 10.9 %collective-permute-start = (bf16[256,128]{1,0:T(8,128)(2,1)}, bf16[256,128]{1,0:T(8,128)(2,1)S(1)}, u32[]{:S(2)}, u32[]{:S(2)}) collective-permute-start(bf16[256,128]{1,0:T(8,128)(2,1)} %param.9), channel_id=1, source_target_pairs={{0,7},{1,8},{2,9},{3,10},{4,11},{5,12},{6,13},{7,14},{8,15},{9,16}... | collective-permute-start | bytes 196616 | tf_op jit(solution)/shard_map/ppermute | solution.py:14
  77.1 28.8 %copy-start.2 = (bf16[2048,128]{1,0:T(8,128)(2,1)}, bf16[2048,128]{1,0:T(8,128)(2,1)S(1)}, u32[]{:S(2)}) copy-start(bf16[2048,128]{1,0:T(8,128)(2,1)S(1)} %constant_dynamic-update-slice_fusion.10) | copy-start | bytes 1572868
  77.9 23.7 %collective-permute-start.1 = (bf16[256,128]{1,0:T(8,128)(2,1)}, bf16[256,128]{1,0:T(8,128)(2,1)S(1)}, u32[]{:S(2)}, u32[]{:S(2)}) collective-permute-start(bf16[256,128]{1,0:T(8,128)(2,1)} %param.9), channel_id=1, source_target_pairs={{0,6},{1,7},{2,8},{3,9},{4,10},{5,11},{6,12},{7,13},{8,14},{9,15},... | collective-permute-start | bytes 196616 | tf_op jit(solution)/shard_map/ppermute | solution.py:14
  101.6 3.5 %collective-permute-start.6 = (bf16[256,128]{1,0:T(8,128)(2,1)}, bf16[256,128]{1,0:T(8,128)(2,1)S(1)}, u32[]{:S(2)}, u32[]{:S(2)}) collective-permute-start(bf16[256,128]{1,0:T(8,128)(2,1)} %param.9), channel_id=1, source_target_pairs={{0,1},{1,2},{2,3},{3,4},{4,5},{5,6},{6,7},{7,8},{8,9},{9,10},{10,1... | collective-permute-start | bytes 196616 | tf_op jit(solution)/shard_map/ppermute | solution.py:14
  108.3 2.4 copy-start.3
  109.5 2.7 %copy-start = (f32[512,2048]{1,0:T(8,128)}, f32[512,2048]{1,0:T(8,128)S(1)}, u32[]{:S(2)}) copy-start(f32[512,2048]{1,0:T(8,128)S(1)} %get-tuple-element.238) | copy-start | bytes 12582916 | tf_op jit(solution)/shard_map/while
  112.3 4.3 %copy-start.1 = (f32[512,2048]{1,0:T(8,128)S(1)}, f32[512,2048]{1,0:T(8,128)}, u32[]{:S(2)}) copy-start(f32[512,2048]{1,0:T(8,128)} %copy-done) | copy-start | bytes 12582916 | tf_op jit(solution)/shard_map/while
  112.4 4.3 %copy-start.4 = (bf16[2048,128]{1,0:T(8,128)(2,1)S(1)}, bf16[2048,128]{1,0:T(8,128)(2,1)}, u32[]{:S(2)}) copy-start(bf16[2048,128]{1,0:T(8,128)(2,1)} %get-tuple-element.282) | copy-start | bytes 1572868 | tf_op jit(solution)/shard_map/while
  123.6 2.4 copy-start.3
  124.7 2.7 %copy-start = (f32[512,2048]{1,0:T(8,128)}, f32[512,2048]{1,0:T(8,128)S(1)}, u32[]{:S(2)}) copy-start(f32[512,2048]{1,0:T(8,128)S(1)} %get-tuple-element.238) | copy-start | bytes 12582916 | tf_op jit(solution)/shard_map/while
  127.6 4.3 %copy-start.1 = (f32[512,2048]{1,0:T(8,128)S(1)}, f32[512,2048]{1,0:T(8,128)}, u32[]{:S(2)}) copy-start(f32[512,2048]{1,0:T(8,128)} %copy-done) | copy-start | bytes 12582916 | tf_op jit(solution)/shard_map/while
  127.6 4.3 %copy-start.4 = (bf16[2048,128]{1,0:T(8,128)(2,1)S(1)}, bf16[2048,128]{1,0:T(8,128)(2,1)}, u32[]{:S(2)}) copy-start(bf16[2048,128]{1,0:T(8,128)(2,1)} %get-tuple-element.282) | copy-start | bytes 1572868 | tf_op jit(solution)/shard_map/while
  138.9 2.4 copy-start.3
  140.0 2.7 %copy-start = (f32[512,2048]{1,0:T(8,128)}, f32[512,2048]{1,0:T(8,128)S(1)}, u32[]{:S(2)}) copy-start(f32[512,2048]{1,0:T(8,128)S(1)} %get-tuple-element.238) | copy-start | bytes 12582916 | tf_op jit(solution)/shard_map/while
  142.9 4.3 %copy-start.1 = (f32[512,2048]{1,0:T(8,128)S(1)}, f32[512,2048]{1,0:T(8,128)}, u32[]{:S(2)}) copy-start(f32[512,2048]{1,0:T(8,128)} %copy-done) | copy-start | bytes 12582916 | tf_op jit(solution)/shard_map/while
  142.9 4.3 %copy-start.4 = (bf16[2048,128]{1,0:T(8,128)(2,1)S(1)}, bf16[2048,128]{1,0:T(8,128)(2,1)}, u32[]{:S(2)}) copy-start(bf16[2048,128]{1,0:T(8,128)(2,1)} %get-tuple-element.282) | copy-start | bytes 1572868 | tf_op jit(solution)/shard_map/while
  154.2 2.4 copy-start.3
  155.3 2.7 %copy-start = (f32[512,2048]{1,0:T(8,128)}, f32[512,2048]{1,0:T(8,128)S(1)}, u32[]{:S(2)}) copy-start(f32[512,2048]{1,0:T(8,128)S(1)} %get-tuple-element.238) | copy-start | bytes 12582916 | tf_op jit(solution)/shard_map/while
  158.2 4.3 %copy-start.1 = (f32[512,2048]{1,0:T(8,128)S(1)}, f32[512,2048]{1,0:T(8,128)}, u32[]{:S(2)}) copy-start(f32[512,2048]{1,0:T(8,128)} %copy-done) | copy-start | bytes 12582916 | tf_op jit(solution)/shard_map/while
  158.2 4.3 %copy-start.4 = (bf16[2048,128]{1,0:T(8,128)(2,1)S(1)}, bf16[2048,128]{1,0:T(8,128)(2,1)}, u32[]{:S(2)}) copy-start(bf16[2048,128]{1,0:T(8,128)(2,1)} %get-tuple-element.282) | copy-start | bytes 1572868 | tf_op jit(solution)/shard_map/while
  167.3 12.5 %collective-permute-start.14 = (bf16[256,128]{1,0:T(8,128)(2,1)S(1)}, bf16[256,128]{1,0:T(8,128)(2,1)S(1)}, u32[]{:S(2)}, u32[]{:S(2)}) collective-permute-start(bf16[256,128]{1,0:T(8,128)(2,1)S(1)} %get-tuple-element.152), channel_id=1, source_target_pairs={{1,0},{2,1},{3,2},{4,3},{5,4},{6,5},{7,6},{8,7},{9,8},{10,9},{11,1... | collective-permute-start | bytes 196616 | tf_op jit(solution)/shard_map/ppermute | solution.py:14
  169.2 14.4 %collective-permute-start.20 = (bf16[256,128]{1,0:T(8,128)(2,1)S(1)}, bf16[256,128]{1,0:T(8,128)(2,1)S(1)}, u32[]{:S(2)}, u32[]{:S(2)}) collective-permute-start(bf16[256,128]{1,0:T(8,128)(2,1)S(1)} %get-tuple-element.153), channel_id=1, source_target_pairs={{7,0},{8,1},{9,2},{10,3},{11,4},{12,5},{13,6},{14,7},{15,8},{16,9}... | collective-permute-start | bytes 196616 | tf_op jit(solution)/shard_map/ppermute | solution.py:14
  171.1 14.4 %collective-permute-start.19 = (bf16[256,128]{1,0:T(8,128)(2,1)S(1)}, bf16[256,128]{1,0:T(8,128)(2,1)S(1)}, u32[]{:S(2)}, u32[]{:S(2)}) collective-permute-start(bf16[256,128]{1,0:T(8,128)(2,1)S(1)} %get-tuple-element.154), channel_id=1, source_target_pairs={{6,0},{7,1},{8,2},{9,3},{10,4},{11,5},{12,6},{13,7},{14,8},{15,9},... | collective-permute-start | bytes 196616 | tf_op jit(solution)/shard_map/ppermute | solution.py:14
  173.1 14.7 %collective-permute-start.18 = (bf16[256,128]{1,0:T(8,128)(2,1)S(1)}, bf16[256,128]{1,0:T(8,128)(2,1)S(1)}, u32[]{:S(2)}, u32[]{:S(2)}) collective-permute-start(bf16[256,128]{1,0:T(8,128)(2,1)S(1)} %get-tuple-element.155), channel_id=1, source_target_pairs={{5,0},{6,1},{7,2},{8,3},{9,4},{10,5},{11,6},{12,7},{13,8},{14,9},{... | collective-permute-start | bytes 196616 | tf_op jit(solution)/shard_map/ppermute | solution.py:14
  177.7 25.3 %collective-permute-start.17 = (bf16[256,128]{1,0:T(8,128)(2,1)S(1)}, bf16[256,128]{1,0:T(8,128)(2,1)S(1)}, u32[]{:S(2)}, u32[]{:S(2)}) collective-permute-start(bf16[256,128]{1,0:T(8,128)(2,1)S(1)} %get-tuple-element.156), channel_id=1, source_target_pairs={{4,0},{5,1},{6,2},{7,3},{8,4},{9,5},{10,6},{11,7},{12,8},{13,9},{1... | collective-permute-start | bytes 196616 | tf_op jit(solution)/shard_map/ppermute | solution.py:14
  179.8 32.8 %collective-permute-start.16 = (bf16[256,128]{1,0:T(8,128)(2,1)S(1)}, bf16[256,128]{1,0:T(8,128)(2,1)S(1)}, u32[]{:S(2)}, u32[]{:S(2)}) collective-permute-start(bf16[256,128]{1,0:T(8,128)(2,1)S(1)} %get-tuple-element.157), channel_id=1, source_target_pairs={{3,0},{4,1},{5,2},{6,3},{7,4},{8,5},{9,6},{10,7},{11,8},{12,9},{13... | collective-permute-start | bytes 196616 | tf_op jit(solution)/shard_map/ppermute | solution.py:14
  183.6 36.7 %collective-permute-start.15 = (bf16[256,128]{1,0:T(8,128)(2,1)S(1)}, bf16[256,128]{1,0:T(8,128)(2,1)S(1)}, u32[]{:S(2)}, u32[]{:S(2)}) collective-permute-start(bf16[256,128]{1,0:T(8,128)(2,1)S(1)} %get-tuple-element.158), channel_id=1, source_target_pairs={{2,0},{3,1},{4,2},{5,3},{6,4},{7,5},{8,6},{9,7},{10,8},{11,9},{12,... | collective-permute-start | bytes 196616 | tf_op jit(solution)/shard_map/ppermute | solution.py:14
  185.6 47.1 %collective-permute-start.21 = (bf16[256,128]{1,0:T(8,128)(2,1)S(1)}, bf16[256,128]{1,0:T(8,128)(2,1)S(1)}, u32[]{:S(2)}, u32[]{:S(2)}) collective-permute-start(bf16[256,128]{1,0:T(8,128)(2,1)S(1)} %get-tuple-element.145), channel_id=1, source_target_pairs={{1,0},{2,1},{3,2},{4,3},{5,4},{6,5},{7,6},{8,7},{9,8},{10,9},{11,1... | collective-permute-start | bytes 196616 | tf_op jit(solution)/shard_map/ppermute | solution.py:14
  187.7 51.2 %collective-permute-start.27 = (bf16[256,128]{1,0:T(8,128)(2,1)S(1)}, bf16[256,128]{1,0:T(8,128)(2,1)S(1)}, u32[]{:S(2)}, u32[]{:S(2)}) collective-permute-start(bf16[256,128]{1,0:T(8,128)(2,1)S(1)} %get-tuple-element.146), channel_id=1, source_target_pairs={{7,0},{8,1},{9,2},{10,3},{11,4},{12,5},{13,6},{14,7},{15,8},{16,9}... | collective-permute-start | bytes 196616 | tf_op jit(solution)/shard_map/ppermute | solution.py:14
  203.0 38.9 %collective-permute-start.26 = (bf16[256,128]{1,0:T(8,128)(2,1)S(1)}, bf16[256,128]{1,0:T(8,128)(2,1)S(1)}, u32[]{:S(2)}, u32[]{:S(2)}) collective-permute-start(bf16[256,128]{1,0:T(8,128)(2,1)S(1)} %get-tuple-element.147), channel_id=1, source_target_pairs={{6,0},{7,1},{8,2},{9,3},{10,4},{11,5},{12,6},{13,7},{14,8},{15,9},... | collective-permute-start | bytes 196616 | tf_op jit(solution)/shard_map/ppermute | solution.py:14
  212.6 29.3 %collective-permute-start.25 = (bf16[256,128]{1,0:T(8,128)(2,1)S(1)}, bf16[256,128]{1,0:T(8,128)(2,1)S(1)}, u32[]{:S(2)}, u32[]{:S(2)}) collective-permute-start(bf16[256,128]{1,0:T(8,128)(2,1)S(1)} %get-tuple-element.148), channel_id=1, source_target_pairs={{5,0},{6,1},{7,2},{8,3},{9,4},{10,5},{11,6},{12,7},{13,8},{14,9},{... | collective-permute-start | bytes 196616 | tf_op jit(solution)/shard_map/ppermute | solution.py:14
  220.3 21.5 %collective-permute-start.24 = (bf16[256,128]{1,0:T(8,128)(2,1)S(1)}, bf16[256,128]{1,0:T(8,128)(2,1)S(1)}, u32[]{:S(2)}, u32[]{:S(2)}) collective-permute-start(bf16[256,128]{1,0:T(8,128)(2,1)S(1)} %get-tuple-element.149), channel_id=1, source_target_pairs={{4,0},{5,1},{6,2},{7,3},{8,4},{9,5},{10,6},{11,7},{12,8},{13,9},{1... | collective-permute-start | bytes 196616 | tf_op jit(solution)/shard_map/ppermute | solution.py:14
  232.7 9.2 %collective-permute-start.23 = (bf16[256,128]{1,0:T(8,128)(2,1)S(1)}, bf16[256,128]{1,0:T(8,128)(2,1)S(1)}, u32[]{:S(2)}, u32[]{:S(2)}) collective-permute-start(bf16[256,128]{1,0:T(8,128)(2,1)S(1)} %get-tuple-element.150), channel_id=1, source_target_pairs={{3,0},{4,1},{5,2},{6,3},{7,4},{8,5},{9,6},{10,7},{11,8},{12,9},{13... | collective-permute-start | bytes 196616 | tf_op jit(solution)/shard_map/ppermute | solution.py:14
  238.9 6.8 %collective-permute-start.22 = (bf16[256,128]{1,0:T(8,128)(2,1)S(1)}, bf16[256,128]{1,0:T(8,128)(2,1)S(1)}, u32[]{:S(2)}, u32[]{:S(2)}) collective-permute-start(bf16[256,128]{1,0:T(8,128)(2,1)S(1)} %get-tuple-element.151), channel_id=1, source_target_pairs={{2,0},{3,1},{4,2},{5,3},{6,4},{7,5},{8,6},{9,7},{10,8},{11,9},{12,... | collective-permute-start | bytes 196616 | tf_op jit(solution)/shard_map/ppermute | solution.py:14
where the time goes:
time: 248 us; the launch traced here: 246 us
  starting transfers between devices  143 us (58%)
  matrix products  42.5 us (17%)
  waiting for transfers between devices  35.7 us (14%)
  local copies, waits for them, and re-layouts  15.1 us (6%)
  other arithmetic  8.33 us (3%)
    ppermute x28, starting transfers between devices, shifted(): lax.ppermute(value, axis, [(source, source + steps) for source in range(f...  143 us
    ppermute x28, waiting for transfers between devices, shifted(): lax.ppermute(value, axis, [(source, source + steps) for source in range(f...  35.7 us
    dot_general x4, matrix products, attend_block(): jnp.dot(probs_bf.T, grad_rows, preferred_element_type=jnp.float32)  16.9 us
    dot_general x4, matrix products, attend_block(): jnp.dot(grad_rows, win_values.T, preferred_element_type=jnp.float32)  8.08 us
    dynamic_slice x8, local copies, waits for them, and re-layouts, local(): lax.scan(fold_step, (empty, empty), (q_blocks, g_blocks, pos_blocks, begi...  7.36 us
    dot_general x4, matrix products, attend_block(): jnp.dot(weights_bf, win_values, preferred_element_type=jnp.float32)  5.59 us
    reduce_sum x4, other arithmetic, attend_block(): row_sum = jnp.sum(weights, axis=2, keepdims=True)  5.11 us
  transfers between devices with their start and end apart: 28, of which 12 were waited for; matrix products, arithmetic and copies ran while one was open for 1% of the time, Pallas kernels for 0%

commit v1 on v0

v1 whole, which is shorter than its diff:
```python
import math

import jax
import jax.numpy as jnp
from jax import lax
from jax.experimental import pallas as pl
from jax.experimental.pallas import tpu as pltpu
from jax.sharding import PartitionSpec as P

REACH = 8
AXES = ("dp", "ctx")
F32 = jnp.float32
BF16 = jnp.bfloat16
BIG = 1e30


def cyclic(value, steps):
    count = lax.axis_size(AXES)
    return lax.ppermute(value, AXES, [(s, (s + steps) % count) for s in range(count)])


def swapped(value, bit):
    count = lax.axis_size(AXES)
    return lax.ppermute(value, AXES, [(s, s ^ bit) for s in range(count)])


def dot(a, b):
    return jnp.dot(a, b, preferred_element_type=F32)


def attend_kernel(
    first_ref, ends_ref, q_ref, g_ref, own_ref, four_ref, two_ref, odd_ref,
    o_ref, dq_ref, even_ref, far_ref,
    kaug, k_t, v_t, f_t, s_ref, w_all, ds_all, q_div, g_div,
):
    tokens, dim = own_ref.shape[1:]
    heads = q_ref.shape[1] // dim
    window = REACH * tokens
    scale = dim ** -0.5
    first = first_ref[0]
    blocks = [
        odd_ref.at[3], two_ref.at[1], odd_ref.at[2], four_ref,
        odd_ref.at[1], two_ref.at[0], odd_ref.at[0], own_ref,
    ]
    ends = ends_ref[0:1, :]
    starts = ends_ref[1:2, :]
    docs = ends_ref.shape[1]
    for b, block in enumerate(blocks):
        rows = slice(b * tokens, (b + 1) * tokens)
        at = first - (REACH - 1 - b) * tokens + lax.broadcasted_iota(jnp.int32, (tokens, docs), 0)
        inside = (at >= starts) & (at < ends)
        kaug[rows, :dim] = block[0]
        kaug[rows, dim:] = jnp.where(inside, 1.0, 0.0).astype(BF16)
        k_t[:, rows] = block[0].T
        v_t[:, rows] = block[1].T
    f_t[...] = jnp.where(inside, 0.0, -BIG).T.astype(BF16)
    causal = lax.broadcasted_iota(jnp.int32, (tokens, tokens), 0) <= lax.broadcasted_iota(
        jnp.int32, (tokens, tokens), 1
    )

    def head(h, carry):
        cols = pl.ds(pl.multiple_of(h * dim, dim), dim)
        span = pl.ds(pl.multiple_of(h * tokens, tokens), tokens)
        q = q_ref[:, cols]
        g = g_ref[:, cols]
        g_t = g.T
        q_aug = jnp.concatenate([q.T, f_t[...]], axis=0)
        top = jnp.full((8, tokens), -jnp.inf, F32)
        for b in range(REACH):
            rows = slice(b * tokens, (b + 1) * tokens)
            s = dot(kaug[rows, :], q_aug)
            if b == REACH - 1:
                s = jnp.where(causal, s, -BIG)
            s_ref[rows, :] = s
            top = jnp.maximum(top, jnp.max(s.reshape(tokens // 8, 8, tokens), axis=0))
        unit = scale * math.log2(math.e)
        row_max = jnp.max(top, axis=0, keepdims=True) * unit
        total = jnp.zeros((8, tokens), F32)
        for b in range(REACH):
            rows = slice(b * tokens, (b + 1) * tokens)
            w = jnp.exp2(s_ref[rows, :] * unit - row_max)
            total = total + jnp.sum(w.reshape(tokens // 8, 8, tokens), axis=0)
            s_ref[rows, :] = w
            w_all[rows, span] = w.astype(BF16)
        inv = 1.0 / jnp.sum(total, axis=0, keepdims=True)
        o_t = dot(v_t[...], w_all[:, span]) * inv
        o_ref[:, cols] = o_t.T.astype(BF16)
        row_dot = jnp.sum(g_t.astype(F32) * o_t.astype(BF16).astype(F32), axis=0, keepdims=True)
        inv_col = jnp.broadcast_to(inv, (dim, tokens)).T
        g_div[span, :] = (g.astype(F32) * inv_col).astype(BF16)
        q_div[span, :] = (q.astype(F32) * inv_col).astype(BF16)
        for b, block in enumerate(blocks):
            rows = slice(b * tokens, (b + 1) * tokens)
            ds = s_ref[rows, :] * (dot(block[1], g_t) - row_dot)
            ds_all[rows, span] = ds.astype(BF16)
        dq_t = dot(k_t[...], ds_all[:, span]) * (inv * scale)
        dq_ref[:, cols] = dq_t.T.astype(BF16)
        return carry

    lax.fori_loop(0, heads, head, 0)
    for b in range(REACH):
        rows = slice(b * tokens, (b + 1) * tokens)
        back = REACH - 1 - b
        out, slot = (far_ref, back // 2) if back % 2 else (even_ref, back // 2)
        out[slot, 0] = (dot(ds_all[rows, :], q_div[...]) * scale).astype(out.dtype)
        out[slot, 1] = dot(w_all[rows, :], g_div[...]).astype(out.dtype)


def attend(first, ends, queries, grad_out, own, four, two, odd):
    tokens, dim = own.shape[1:]
    width = queries.shape[1]
    heads = width // dim
    window = REACH * tokens
    vmem = pl.BlockSpec(memory_space=pltpu.VMEM)
    half = REACH // 2
    return pl.pallas_call(
        attend_kernel,
        out_shape=(
            jax.ShapeDtypeStruct((tokens, width), BF16),
            jax.ShapeDtypeStruct((tokens, width), BF16),
            jax.ShapeDtypeStruct((half, 2, tokens, dim), F32),
            jax.ShapeDtypeStruct((half, 2, tokens, dim), BF16),
        ),
        in_specs=[pl.BlockSpec(memory_space=pltpu.SMEM)] + [vmem] * 7,
        out_specs=(vmem,) * 4,
        scratch_shapes=[
            pltpu.VMEM((window, 2 * dim), BF16),
            pltpu.VMEM((dim, window), BF16),
            pltpu.VMEM((dim, window), BF16),
            pltpu.VMEM((dim, tokens), BF16),
            pltpu.VMEM((window, tokens), F32),
            pltpu.VMEM((window, heads * tokens), BF16),
            pltpu.VMEM((window, heads * tokens), BF16),
            pltpu.VMEM((heads * tokens, dim), BF16),
            pltpu.VMEM((heads * tokens, dim), BF16),
        ],
        compiler_params=pltpu.CompilerParams(vmem_limit_bytes=56 * 2**20),
    )(first, ends, queries, grad_out, own, four, two, odd)


def local(doc_lengths, queries, key_rows, value_rows, grad_out):
    rows_dev = queries.shape[0]
    dev_rank = lax.axis_index(AXES)
    first_row = (dev_rank * rows_dev).astype(jnp.int32).reshape(1)
    doc_ends = jnp.cumsum(doc_lengths).astype(jnp.int32)
    spare = 128 - doc_lengths.shape[0]
    bounds = jnp.stack(
        [
            jnp.pad(doc_ends, (0, spare)),
            jnp.pad(doc_ends - doc_lengths, (0, spare), constant_values=-(2**30)),
        ]
    )
    bounds = jnp.pad(bounds, ((0, 6), (0, 0)))
    upper_core = dev_rank % 2 == 1
    upper_chip = dev_rank // 2 % 2 == 1

    own = jnp.stack([key_rows, value_rows])
    four = cyclic(own, 4)
    eight = cyclic(own, 8)
    two = swapped(
        jnp.where(upper_chip, jnp.stack([four, eight]), jnp.stack([own, four])), 2
    )
    odd = swapped(
        jnp.where(
            upper_core,
            jnp.stack([two[0], four, two[1], eight]),
            jnp.stack([own, two[0], four, two[1]]),
        ),
        1,
    )
    attn_out, grad_queries, even, far = attend(
        first_row, bounds, queries, grad_out, own, four, two, odd
    )
    back = swapped(far, 1).astype(F32)
    none = jnp.zeros_like(even[:1])
    even = jnp.concatenate([even, none]) + jnp.where(
        upper_core, jnp.concatenate([none, back]), jnp.concatenate([back, none])
    )
    back = swapped(jnp.stack([even[1], even[3]]).astype(BF16), 2).astype(F32)
    sum_zero = even[0] + jnp.where(upper_chip, 0.0, back[0])
    sum_four = even[2] + jnp.where(upper_chip, back[0], back[1])
    sum_eight = even[4] + jnp.where(upper_chip, back[1], 0.0)
    sums = (
        sum_zero
        + cyclic(sum_four.astype(BF16), -4).astype(F32)
        + cyclic(sum_eight.astype(BF16), -8).astype(F32)
    ).astype(BF16)
    return (attn_out, grad_queries, sums[0], sums[1])


def solution(mesh):
    split = P(AXES, None)
    return jax.shard_map(
        local,
        mesh=mesh,
        in_specs=(P(), split, split, split, split),
        out_specs=(split,) * 4,
        check_vma=False,
    )
```

time: 248 us -> 86.5 us (0.35)
  the two profiles are of different devices: /device:TPU:167 before, /device:TPU:86 now
where the time goes in v1:
time: 86.5 us; the launch traced here: 86.3 us
  waiting for transfers between devices  43.2 us (50%)
  Pallas kernels  25.9 us (30%)
  starting transfers between devices  12.5 us (14%)
  local copies, waits for them, and re-layouts  2.23 us (3%)
  other arithmetic  1.79 us (2%)
    ppermute x4, waiting for transfers between devices, cyclic(): lax.ppermute(value, AXES, [(s, (s + steps) % count) for s in range(count)])  27.5 us
    pallas_call x1, Pallas kernels, attend(): pl.pallas_call(attend_kernel, out_shape=(jax.ShapeDtypeStruct((tokens, wi...  25.9 us
    ppermute x4, waiting for transfers between devices, swapped(): return lax.ppermute(value, AXES, [(s, s ^ bit) for s in range(count)])  15.7 us
    ppermute x4, starting transfers between devices, cyclic(): lax.ppermute(value, AXES, [(s, (s + steps) % count) for s in range(count)])  8.89 us
    ppermute x4, starting transfers between devices, swapped(): return lax.ppermute(value, AXES, [(s, s ^ bit) for s in range(count)])  3.59 us
  transfers between devices with their start and end apart: 8, of which 8 were waited for; matrix products, arithmetic and copies ran while one was open for 1% of the time, Pallas kernels for 0%

profile of v1, /device:TPU:86, one launch (start us, length us, event | category | flops | bytes accessed | tf_op | source)
XLA Modules:
  0.0 86.3 jit_solution(10662904339057894278)
XLA Ops:
  0.6 0.9 %fusion.8 = (bf16[1,2,256,128]{3,2,1,0:T(8,128)(2,1)S(1)}, bf16[2,256,128]{2,1,0:T(8,128)(2,1)S(1)}) fusion(bf16[1,256,128]{2,1,0:T(8,128)(2,1)} %bitcast.32, bf16[1,256,128]{2,1,0:T(8,128)(2,1)} %bitcast.33), kind=kLoop, calls=%fused_computation.21 | loop fusion | flops 65536 | bytes 393216 | tf_op jit(solution)/shard_map/stack | solution.py:161
  1.5 0.0 copy-start.4
  1.5 0.0 copy-start.5
  1.5 4.2 %collective-permute-start.1 = (bf16[2,256,128]{2,1,0:T(8,128)(2,1)S(1)}, bf16[2,256,128]{2,1,0:T(8,128)(2,1)S(1)}, u32[]{:S(2)}, u32[]{:S(2)}) collective-permute-start(bf16[2,256,128]{2,1,0:T(8,128)(2,1)S(1)} %get-tuple-element.23.own_ref), channel_id=1, source_target_pairs={{0,8},{1,9},{2,10},{3,11},{4,12},{5,13},{6,14},{7,15},{8,16},{9,17... | collective-permute-start | bytes 393224 | tf_op jit(solution)/shard_map/ppermute | solution.py:19
  5.8 2.2 %collective-permute-start = (bf16[2,256,128]{2,1,0:T(8,128)(2,1)S(1)}, bf16[2,256,128]{2,1,0:T(8,128)(2,1)S(1)}, u32[]{:S(2)}, u32[]{:S(2)}) collective-permute-start(bf16[2,256,128]{2,1,0:T(8,128)(2,1)S(1)} %get-tuple-element.23.own_ref), channel_id=1, source_target_pairs={{0,4},{1,5},{2,6},{3,7},{4,8},{5,9},{6,10},{7,11},{8,12},{9,13},{1... | collective-permute-start | bytes 393224 | tf_op jit(solution)/shard_map/ppermute | solution.py:19
  8.0 3.3 %collective-permute-done.1 = bf16[2,256,128]{2,1,0:T(8,128)(2,1)S(1)} collective-permute-done((bf16[2,256,128]{2,1,0:T(8,128)(2,1)S(1)}, bf16[2,256,128]{2,1,0:T(8,128)(2,1)S(1)}, u32[]{:S(2)}, u32[]{:S(2)}) %collective-permute-start.1) | collective-permute-done | bytes 131104 | tf_op jit(solution)/shard_map/ppermute | solution.py:19
  11.3 0.3 collective-permute-done.four_ref
  11.5 0.0 copy-start
  11.6 1.6 %collective-permute-start.2 = (bf16[2,2,256,128]{3,2,1,0:T(8,128)(2,1)S(1)}, bf16[2,2,256,128]{3,2,1,0:T(8,128)(2,1)S(1)}, u32[]{:S(2)}, u32[]{:S(2)}) collective-permute-start(bf16[2,2,256,128]{3,2,1,0:T(8,128)(2,1)S(1)} %maximum_select_fusion.1), channel_id=1, source_target_pairs={{0,2},{1,3},{2,0},{3,1},{4,6},{5,7},{6,4},{7,5},{8,10},{9,11},{10,... | collective-permute-start | bytes 786440 | tf_op jit(solution)/shard_map/ppermute | solution.py:24
  13.2 6.0 %collective-permute-done.2.two_ref = bf16[2,2,256,128]{3,2,1,0:T(8,128)(2,1)S(1)} collective-permute-done((bf16[2,2,256,128]{3,2,1,0:T(8,128)(2,1)S(1)}, bf16[2,2,256,128]{3,2,1,0:T(8,128)(2,1)S(1)}, u32[]{:S(2)}, u32[]{:S(2)}) %collective-permute-start.2) | collective-permute-done | bytes 262176 | tf_op jit(solution)/shard_map/ppermute | solution.py:24
  19.2 0.0 copy-start.1
  19.3 0.1 maximum_select_fusion
  19.4 0.1 collective-permute-start.3
  19.5 0.0 copy-done.5
  19.5 0.1 copy.10
  19.6 0.1 reduce-window.9
  19.7 0.1 reduce
  19.8 0.6 pad.16.ends_ref
  20.4 0.9 %collective-permute-done.3.odd_ref = bf16[4,2,256,128]{3,2,1,0:T(8,128)(2,1)S(1)} collective-permute-done((bf16[4,2,256,128]{3,2,1,0:T(8,128)(2,1)S(1)}, bf16[4,2,256,128]{3,2,1,0:T(8,128)(2,1)S(1)}, u32[]{:S(2)}, u32[]{:S(2)}) %collective-permute-start.3) | collective-permute-done | bytes 524320 | tf_op jit(solution)/shard_map/ppermute | solution.py:24
  21.4 0.0 copy-start.3
  21.4 0.0 copy-done.4
  21.4 0.0 copy-done
  21.4 0.0 copy-done.1
  21.4 0.8 copy-done.3
  22.2 25.9 %shard_map.84 = (bf16[256,1024]{1,0:T(8,128)(2,1)}, bf16[256,1024]{1,0:T(8,128)(2,1)}, f32[4,2,256,128]{3,2,1,0:T(8,128)}, bf16[4,2,256,128]{3,2,1,0:T(8,128)(2,1)}) custom-call(s32[1]{0:T(128)} %bitcast.first_ref, s32[8,128]{1,0:T(8,128)} %pad.16.ends_ref, bf16[256,1024]{1,0:T(8,128)(2,1)} %q_ref.1, bf16[256,1024]{1,0:T(8,128)(2,1)} %g_ref.1, ...), custom_call_target="tpu_custom_call" | custom-call | tf_op jit(solution)/shard_map/pallas_call | solution.py:116
  48.1 0.0 copy-start.2
  48.1 0.1 collective-permute-start.4
  48.2 2.0 %collective-permute-done.4 = bf16[4,2,256,128]{3,2,1,0:T(8,128)(2,1)S(1)} collective-permute-done((bf16[4,2,256,128]{3,2,1,0:T(8,128)(2,1)}, bf16[4,2,256,128]{3,2,1,0:T(8,128)(2,1)S(1)}, u32[]{:S(2)}, u32[]{:S(2)}) %collective-permute-start.4) | collective-permute-done | bytes 524320 | tf_op jit(solution)/shard_map/ppermute | solution.py:24
  50.2 0.1 convert_element_type.28
  50.3 0.0 copy-done.2
  50.3 0.2 fusion.9
  50.6 1.7 %collective-permute-start.5 = (bf16[2,2,256,128]{3,2,1,0:T(8,128)(2,1)S(1)}, bf16[2,2,256,128]{3,2,1,0:T(8,128)(2,1)S(1)}, u32[]{:S(2)}, u32[]{:S(2)}) collective-permute-start(bf16[2,2,256,128]{3,2,1,0:T(8,128)(2,1)S(1)} %pad_maximum_fusion), channel_id=1, source_target_pairs={{0,2},{1,3},{2,0},{3,1},{4,6},{5,7},{6,4},{7,5},{8,10},{9,11},{10,... | collective-permute-start | bytes 786440 | tf_op jit(solution)/shard_map/ppermute | solution.py:24
  52.3 6.7 %collective-permute-done.5 = bf16[2,2,256,128]{3,2,1,0:T(8,128)(2,1)S(1)} collective-permute-done((bf16[2,2,256,128]{3,2,1,0:T(8,128)(2,1)S(1)}, bf16[2,2,256,128]{3,2,1,0:T(8,128)(2,1)S(1)}, u32[]{:S(2)}, u32[]{:S(2)}) %collective-permute-start.5) | collective-permute-done | bytes 262176 | tf_op jit(solution)/shard_map/ppermute | solution.py:24
  59.1 0.1 fusion.6
  59.2 0.1 collective-permute-start.6
  59.2 2.4 %collective-permute-start.7 = (bf16[2,256,128]{2,1,0:T(8,128)(2,1)S(1)}, bf16[2,256,128]{2,1,0:T(8,128)(2,1)S(1)}, u32[]{:S(2)}, u32[]{:S(2)}) collective-permute-start(bf16[2,256,128]{2,1,0:T(8,128)(2,1)S(1)} %get-tuple-element.15), channel_id=1, source_target_pairs={{0,248},{1,249},{2,250},{3,251},{4,252},{5,253},{6,254},{7,255},{8... | collective-permute-start | bytes 393224 | tf_op jit(solution)/shard_map/ppermute | solution.py:19
  61.6 9.3 %collective-permute-done.6 = bf16[2,256,128]{2,1,0:T(8,128)(2,1)S(1)} collective-permute-done((bf16[2,256,128]{2,1,0:T(8,128)(2,1)S(1)}, bf16[2,256,128]{2,1,0:T(8,128)(2,1)S(1)}, u32[]{:S(2)}, u32[]{:S(2)}) %collective-permute-start.6) | collective-permute-done | bytes 131104 | tf_op jit(solution)/shard_map/ppermute | solution.py:19
  70.9 14.6 %collective-permute-done.7 = bf16[2,256,128]{2,1,0:T(8,128)(2,1)S(1)} collective-permute-done((bf16[2,256,128]{2,1,0:T(8,128)(2,1)S(1)}, bf16[2,256,128]{2,1,0:T(8,128)(2,1)S(1)}, u32[]{:S(2)}, u32[]{:S(2)}) %collective-permute-start.7) | collective-permute-done | bytes 131104 | tf_op jit(solution)/shard_map/ppermute | solution.py:19
  85.6 0.1 fusion.5
  85.7 0.7 slice_bitcast_fusion
  (8 shorter events, 0.2 us)
Async XLA Ops:
  1.5 19.9 %copy-start.4 = (bf16[2,256,128]{2,1,0:T(8,128)(2,1)}, bf16[2,256,128]{2,1,0:T(8,128)(2,1)S(1)}, u32[]{:S(2)}) copy-start(bf16[2,256,128]{2,1,0:T(8,128)(2,1)S(1)} %get-tuple-element.23.own_ref) | copy-start | bytes 393220
  1.5 17.9 %copy-start.5 = (s32[64]{0:T(128)S(1)}, s32[64]{0:T(128)}, u32[]{:S(2)}) copy-start(s32[64]{0:T(128)} %param.5) | copy-start | bytes 772
  1.5 9.7 %collective-permute-start.1 = (bf16[2,256,128]{2,1,0:T(8,128)(2,1)S(1)}, bf16[2,256,128]{2,1,0:T(8,128)(2,1)S(1)}, u32[]{:S(2)}, u32[]{:S(2)}) collective-permute-start(bf16[2,256,128]{2,1,0:T(8,128)(2,1)S(1)} %get-tuple-element.23.own_ref), channel_id=1, source_target_pairs={{0,8},{1,9},{2,10},{3,11},{4,12},{5,13},{6,14},{7,15},{8,16},{9,17... | collective-permute-start | bytes 393224 | tf_op jit(solution)/shard_map/ppermute | solution.py:19
  5.8 5.7 %collective-permute-start = (bf16[2,256,128]{2,1,0:T(8,128)(2,1)S(1)}, bf16[2,256,128]{2,1,0:T(8,128)(2,1)S(1)}, u32[]{:S(2)}, u32[]{:S(2)}) collective-permute-start(bf16[2,256,128]{2,1,0:T(8,128)(2,1)S(1)} %get-tuple-element.23.own_ref), channel_id=1, source_target_pairs={{0,4},{1,5},{2,6},{3,7},{4,8},{5,9},{6,10},{7,11},{8,12},{9,13},{1... | collective-permute-start | bytes 393224 | tf_op jit(solution)/shard_map/ppermute | solution.py:19
  11.5 9.8 %copy-start = (bf16[2,256,128]{2,1,0:T(8,128)(2,1)}, bf16[2,256,128]{2,1,0:T(8,128)(2,1)S(1)}, u32[]{:S(2)}) copy-start(bf16[2,256,128]{2,1,0:T(8,128)(2,1)S(1)} %collective-permute-done.four_ref) | copy-start | bytes 393220
  11.6 7.7 %collective-permute-start.2 = (bf16[2,2,256,128]{3,2,1,0:T(8,128)(2,1)S(1)}, bf16[2,2,256,128]{3,2,1,0:T(8,128)(2,1)S(1)}, u32[]{:S(2)}, u32[]{:S(2)}) collective-permute-start(bf16[2,2,256,128]{3,2,1,0:T(8,128)(2,1)S(1)} %maximum_select_fusion.1), channel_id=1, source_target_pairs={{0,2},{1,3},{2,0},{3,1},{4,6},{5,7},{6,4},{7,5},{8,10},{9,11},{10,... | collective-permute-start | bytes 786440 | tf_op jit(solution)/shard_map/ppermute | solution.py:24
  19.2 2.2 %copy-start.1 = (bf16[2,2,256,128]{3,2,1,0:T(8,128)(2,1)}, bf16[2,2,256,128]{3,2,1,0:T(8,128)(2,1)S(1)}, u32[]{:S(2)}) copy-start(bf16[2,2,256,128]{3,2,1,0:T(8,128)(2,1)S(1)} %collective-permute-done.2.two_ref) | copy-start | bytes 786436
  19.4 2.0 %collective-permute-start.3 = (bf16[4,2,256,128]{3,2,1,0:T(8,128)(2,1)S(1)}, bf16[4,2,256,128]{3,2,1,0:T(8,128)(2,1)S(1)}, u32[]{:S(2)}, u32[]{:S(2)}) collective-permute-start(bf16[4,2,256,128]{3,2,1,0:T(8,128)(2,1)S(1)} %maximum_select_fusion), channel_id=1, source_target_pairs={{0,1},{1,0},{2,3},{3,2},{4,5},{5,4},{6,7},{7,6},{8,9},{9,8},{10,11... | collective-permute-start | bytes 1572872 | tf_op jit(solution)/shard_map/ppermute | solution.py:24
  21.4 0.8 copy-start.3
  48.1 2.2 %copy-start.2 = (f32[4,2,256,128]{3,2,1,0:T(8,128)S(1)}, f32[4,2,256,128]{3,2,1,0:T(8,128)}, u32[]{:S(2)}) copy-start(f32[4,2,256,128]{3,2,1,0:T(8,128)} %get-tuple-element.10) | copy-start | bytes 3145732
  48.1 2.1 %collective-permute-start.4 = (bf16[4,2,256,128]{3,2,1,0:T(8,128)(2,1)}, bf16[4,2,256,128]{3,2,1,0:T(8,128)(2,1)S(1)}, u32[]{:S(2)}, u32[]{:S(2)}) collective-permute-start(bf16[4,2,256,128]{3,2,1,0:T(8,128)(2,1)} %get-tuple-element.11), channel_id=1, source_target_pairs={{0,1},{1,0},{2,3},{3,2},{4,5},{5,4},{6,7},{7,6},{8,9},{9,8},{10,11... | collective-permute-start | bytes 1572872 | tf_op jit(solution)/shard_map/ppermute | solution.py:24
  50.6 8.4 %collective-permute-start.5 = (bf16[2,2,256,128]{3,2,1,0:T(8,128)(2,1)S(1)}, bf16[2,2,256,128]{3,2,1,0:T(8,128)(2,1)S(1)}, u32[]{:S(2)}, u32[]{:S(2)}) collective-permute-start(bf16[2,2,256,128]{3,2,1,0:T(8,128)(2,1)S(1)} %pad_maximum_fusion), channel_id=1, source_target_pairs={{0,2},{1,3},{2,0},{3,1},{4,6},{5,7},{6,4},{7,5},{8,10},{9,11},{10,... | collective-permute-start | bytes 786440 | tf_op jit(solution)/shard_map/ppermute | solution.py:24
  59.2 11.8 %collective-permute-start.6 = (bf16[2,256,128]{2,1,0:T(8,128)(2,1)S(1)}, bf16[2,256,128]{2,1,0:T(8,128)(2,1)S(1)}, u32[]{:S(2)}, u32[]{:S(2)}) collective-permute-start(bf16[2,256,128]{2,1,0:T(8,128)(2,1)S(1)} %get-tuple-element.14), channel_id=1, source_target_pairs={{0,252},{1,253},{2,254},{3,255},{4,0},{5,1},{6,2},{7,3},{8,4},{9,5... | collective-permute-start | bytes 393224 | tf_op jit(solution)/shard_map/ppermute | solution.py:19
  59.2 26.3 %collective-permute-start.7 = (bf16[2,256,128]{2,1,0:T(8,128)(2,1)S(1)}, bf16[2,256,128]{2,1,0:T(8,128)(2,1)S(1)}, u32[]{:S(2)}, u32[]{:S(2)}) collective-permute-start(bf16[2,256,128]{2,1,0:T(8,128)(2,1)S(1)} %get-tuple-element.15), channel_id=1, source_target_pairs={{0,248},{1,249},{2,250},{3,251},{4,252},{5,253},{6,254},{7,255},{8... | collective-permute-start | bytes 393224 | tf_op jit(solution)/shard_map/ppermute | solution.py:19

commit v2 on v0

v2 whole, which is shorter than its diff:
```python
import functools
import math

import jax
import jax.numpy as jnp
from jax import lax
from jax.experimental import pallas as pl
from jax.experimental.pallas import tpu as pltpu
from jax.sharding import PartitionSpec as P

REACH = 8
AXES = ("dp", "ctx")
F32 = jnp.float32
BF16 = jnp.bfloat16
BIG = 1e30
SHAPE = jax.ShapeDtypeStruct


def cyclic(value, steps):
    count = lax.axis_size(AXES)
    return lax.ppermute(value, AXES, [(s, (s + steps) % count) for s in range(count)])


def swapped(value, bit):
    count = lax.axis_size(AXES)
    return lax.ppermute(value, AXES, [(s, s ^ bit) for s in range(count)])


def dot(a, b):
    return jnp.dot(a, b, preferred_element_type=F32)


def docs_kernel(place_ref, lengths_ref, docs_ref, mask_ref, gates_ref):
    tokens = docs_ref.shape[1]
    docs = lengths_ref.shape[0]
    gate = lax.broadcasted_iota(jnp.int32, gates_ref.shape, 0)
    gates_ref[...] = jnp.where(gate == 0, place_ref[1], place_ref[2]).astype(F32)
    lane = lax.broadcasted_iota(jnp.int32, gates_ref.shape, 1)
    starts = jnp.zeros(lane.shape, jnp.int32)
    ends = jnp.zeros(lane.shape, jnp.int32)
    for doc in range(docs):
        starts = starts + jnp.where(lane > doc, lengths_ref[doc], 0)
        ends = ends + jnp.where(lane >= doc, lengths_ref[doc], 0)
    starts = jnp.where(lane < docs, starts, -(2**30))[:1]
    ends = jnp.where(lane < docs, ends, 0)[:1]
    for back in range(REACH - 1, -1, -1):
        rows = lax.broadcasted_iota(jnp.int32, docs_ref.shape[1:], 0)
        at = place_ref[0] - back * tokens + rows
        inside = (at >= starts) & (at < ends)
        docs_ref[back] = jnp.where(inside, 1.0, 0.0).astype(BF16)
    mask_ref[...] = jnp.where(inside, 0.0, -BIG).T.astype(BF16)


def prep_kernel(mask_ref, q_ref, g_ref, k_ref, v_ref, qa_ref, gt_ref, k_own_ref, v_own_ref):
    tokens, dim = k_ref.shape
    k_own_ref[...] = k_ref[...]
    v_own_ref[...] = v_ref[...]
    for h in range(q_ref.shape[1] // dim):
        cols, span = slice(h * dim, (h + 1) * dim), slice(h * tokens, (h + 1) * tokens)
        qa_ref[:dim, span] = q_ref[:, cols].T
        qa_ref[dim:, span] = mask_ref[...]
        gt_ref[:, span] = g_ref[:, cols].T


def weigh_kernel(backs, groups, docs_ref, qa_ref, *refs):
    w_ref, top_ref, sum_ref, s_ref = refs[-4:]
    block_refs = refs[:groups]
    heads, tokens = top_ref.shape
    dim = qa_ref.shape[0] // 2
    blocks = [r.at[i] for r in block_refs for i in range(r.shape[0])]
    causal = lax.broadcasted_iota(jnp.int32, (tokens, tokens), 0) <= lax.broadcasted_iota(
        jnp.int32, (tokens, tokens), 1
    )
    unit = dim**-0.5 * math.log2(math.e)
    for h in range(heads):
        span = slice(h * tokens, (h + 1) * tokens)
        top = jnp.full((8, tokens), -jnp.inf, F32)
        for b, (back, block) in enumerate(zip(backs, blocks)):
            rows = slice(b * tokens, (b + 1) * tokens)
            s = dot(jnp.concatenate([block[...], docs_ref[back]], axis=1), qa_ref[:, span])
            if back == 0:
                s = jnp.where(causal, s, -BIG)
            s_ref[h % 2, rows, :] = s
            top = jnp.maximum(top, jnp.max(s.reshape(tokens // 8, 8, tokens), axis=0))
        row_max = jnp.max(top, axis=0, keepdims=True) * unit
        top_ref[h : h + 1, :] = row_max
        total = jnp.zeros((8, tokens), F32)
        for b in range(len(backs)):
            rows = slice(b * tokens, (b + 1) * tokens)
            w = jnp.exp2(s_ref[h % 2, rows, :] * unit - row_max)
            total = total + jnp.sum(w.reshape(tokens // 8, 8, tokens), axis=0)
            w_ref[rows, span] = w.astype(BF16)
        sum_ref[h : h + 1, :] = jnp.sum(total, axis=0, keepdims=True)


def value_kernel(
    wa_ref, wb_ref, wc_ref, ta_ref, tb_ref, tc_ref, la_ref, lb_ref, lc_ref, q_ref, g_ref, order_ref,
    coef_ref, qa_ref, qb_ref, qc_ref, even_ref, far_ref, g_div, flat,
):
    heads, tokens = ta_ref.shape
    dim = q_ref.shape[1] // heads
    row_max = jnp.maximum(jnp.maximum(ta_ref[...], tb_ref[...]), tc_ref[...])
    parts = [jnp.exp2(t[...] - row_max) for t in (ta_ref, tb_ref, tc_ref)]
    row_sum = sum(p * l[...] for p, l in zip(parts, (la_ref, lb_ref, lc_ref)))
    inverse = 1.0 / row_sum
    flat[...] = jnp.zeros_like(flat)
    for i, part in enumerate(parts):
        coef_ref[i] = part * inverse
        flat[i * heads : (i + 1) * heads, :] = part * inverse
    columns = flat[...].T
    for h in range(heads):
        cols, span = slice(h * dim, (h + 1) * dim), slice(h * tokens, (h + 1) * tokens)
        q = q_ref[:, cols].astype(F32) * dim**-0.5
        g = g_ref[:, cols].astype(F32)
        for i, qd_ref in enumerate((qa_ref, qb_ref, qc_ref)):
            column = columns[:, i * heads + h : i * heads + h + 1]
            qd_ref[span, :] = (q * column).astype(BF16)
            g_div[i, span, :] = (g * column).astype(BF16)
    for slot in range(REACH // 2):
        rows = slice(slot * tokens, (slot + 1) * tokens)
        far_ref[slot] = dot(wc_ref[rows, :], g_div[2]).astype(BF16)
    for slot in range(2):
        rows = slice(slot * tokens, (slot + 1) * tokens)
        even_ref[2 * slot + 1] = dot(wb_ref[rows, :], g_div[1])
        even_ref[2 * slot] = dot(wa_ref[rows, :], g_div[0])


def out_kernel(wa_ref, wb_ref, wc_ref, coef_ref, gt_ref, own_ref, four_ref, two_ref, odd_ref,
               o_ref, dot_ref, v_t):
    heads, tokens = coef_ref.shape[1:]
    dim = own_ref.shape[2]
    refs = (own_ref, four_ref, two_ref, odd_ref)
    for b, block in enumerate([r.at[i] for r in refs for i in range(r.shape[0])]):
        v_t[:, b * tokens : (b + 1) * tokens] = block[...].T
    for h in range(heads):
        cols, span = slice(h * dim, (h + 1) * dim), slice(h * tokens, (h + 1) * tokens)
        start, out = 0, 0.0
        for i, w_ref in enumerate((wa_ref, wb_ref, wc_ref)):
            stop = start + w_ref.shape[0]
            out = out + dot(v_t[:, start:stop], w_ref[:, span]) * coef_ref[i, h : h + 1, :]
            start = stop
        out = out.astype(BF16)
        o_ref[:, cols] = out.T
        dot_ref[h : h + 1, :] = jnp.sum(
            gt_ref[:, span].astype(F32) * out.astype(F32), axis=0, keepdims=True
        )


def score_terms(w_ref, gt_ref, dot_ref, qd_ref, blocks, ds_ref, outs):
    heads, tokens = dot_ref.shape
    for h in range(heads):
        span = slice(h * tokens, (h + 1) * tokens)
        for b, block in enumerate(blocks):
            rows = slice(b * tokens, (b + 1) * tokens)
            lean = dot(block[...], gt_ref[:, span]) - dot_ref[h : h + 1, :]
            ds_ref[rows, span] = (w_ref[rows, span].astype(F32) * lean).astype(BF16)
    for b, out in enumerate(outs):
        rows = slice(b * tokens, (b + 1) * tokens)
        out[...] = dot(ds_ref[rows, :], qd_ref[...]).astype(out.dtype)


def joined(upper, even, back):
    half = REACH // 2
    terms = [back[j].astype(F32) for j in range(half)]
    first = even[0] + jnp.where(upper, 0.0, terms[0])
    last = jnp.where(upper, terms[half - 1], 0.0)
    return [first] + [
        even[j] + jnp.where(upper, terms[j - 1], terms[j]) for j in range(1, half)
    ] + [last]


def far_kernel(gates_ref, w_ref, gt_ref, dot_ref, qd_ref, odd_ref, even_ref, back_ref,
               ds_ref, far_ref, send_ref, rest_ref):
    half = REACH // 2
    score_terms(
        w_ref, gt_ref, dot_ref, qd_ref, [odd_ref.at[i] for i in range(half)], ds_ref,
        [far_ref.at[i] for i in range(half)],
    )
    sums = joined(gates_ref[0:1, :] > 0, even_ref, back_ref)
    for i in range(2):
        send_ref[i] = sums[2 * i + 1].astype(BF16)
    for i in range(3):
        rest_ref[i] = sums[2 * i]


def mid_kernel(w_ref, gt_ref, dot_ref, qd_ref, two_ref, ds_ref, mid_ref):
    score_terms(
        w_ref, gt_ref, dot_ref, qd_ref, [two_ref.at[i] for i in range(2)], ds_ref,
        [mid_ref.at[i] for i in range(2)],
    )


def near_kernel(w_ref, gt_ref, dot_ref, qd_ref, own_ref, four_ref, order_ref, ds_ref, near_ref):
    score_terms(
        w_ref, gt_ref, dot_ref, qd_ref, [own_ref.at[0], four_ref.at[0]], ds_ref,
        [near_ref.at[i] for i in range(2)],
    )


def pair_kernel(gates_ref, own_ref, four_ref, eight_ref, order_ref, send_ref):
    upper = gates_ref[1:2, :] > 0
    send_ref[0] = jnp.where(upper, four_ref[...].astype(F32), own_ref[...].astype(F32)).astype(BF16)
    send_ref[1] = jnp.where(upper, eight_ref[...].astype(F32), four_ref[...].astype(F32)).astype(BF16)


def quad_kernel(gates_ref, own_ref, four_ref, eight_ref, two_ref, order_ref, send_ref):
    upper = gates_ref[0:1, :] > 0
    blocks = [own_ref, two_ref.at[0], four_ref, two_ref.at[1], eight_ref]
    wide = [block[...].astype(F32) for block in blocks]
    for i in range(REACH // 2):
        send_ref[i] = jnp.where(upper, wide[i + 1], wide[i]).astype(BF16)


def join_kernel(gates_ref, mid_ref, back_ref, send_ref):
    upper = gates_ref[0:1, :] > 0
    for i in range(2):
        back = jnp.where(upper, back_ref[2 * i].astype(F32), back_ref[2 * i + 1].astype(F32))
        send_ref[i] = (mid_ref[i] + back).astype(BF16)


def close_kernel(gates_ref, rest_ref, back_ref, order_ref, zero_ref, four_ref, eight_ref):
    upper = gates_ref[1:2, :] > 0
    back = [back_ref[i].astype(F32) for i in range(2)]
    zero_ref[...] = rest_ref[0] + jnp.where(upper, 0.0, back[0])
    four_ref[...] = (rest_ref[1] + jnp.where(upper, back[0], back[1])).astype(BF16)
    eight_ref[...] = (rest_ref[2] + jnp.where(upper, back[1], 0.0)).astype(BF16)


def near_close_kernel(gates_ref, near_ref, core_ref, chip_ref, order_ref, zero_ref, four_ref, eight_ref):
    other = gates_ref[0:1, :] > 0
    core = [core_ref[i].astype(F32) for i in range(REACH // 2)]
    upper = gates_ref[1:2, :] > 0
    back = [chip_ref[i].astype(F32) for i in range(2)]
    zero_ref[...] = near_ref[0] + jnp.where(other, 0.0, core[0]) + jnp.where(upper, 0.0, back[0])
    four = near_ref[1] + jnp.where(other, core[1], core[2])
    four_ref[...] = (four + jnp.where(upper, back[0], back[1])).astype(BF16)
    eight = jnp.where(other, core[3], 0.0)
    eight_ref[...] = (eight + jnp.where(upper, back[1], 0.0)).astype(BF16)


def query_kernel(
    da_ref, db_ref, dc_ref, coef_ref, own_ref, four_ref, two_ref, odd_ref, order_ref, dq_ref, k_t
):
    heads, tokens = coef_ref.shape[1:]
    dim = own_ref.shape[2]
    refs = (own_ref, four_ref, two_ref, odd_ref)
    for b, block in enumerate([r.at[i] for r in refs for i in range(r.shape[0])]):
        k_t[:, b * tokens : (b + 1) * tokens] = block[...].T
    for h in range(heads):
        cols, span = slice(h * dim, (h + 1) * dim), slice(h * tokens, (h + 1) * tokens)
        start, out = 0, 0.0
        for i, ds_ref in enumerate((da_ref, db_ref, dc_ref)):
            stop = start + ds_ref.shape[0]
            out = out + dot(k_t[:, start:stop], ds_ref[:, span]) * coef_ref[i, h : h + 1, :]
            start = stop
        dq_ref[:, cols] = (out * dim**-0.5).T.astype(BF16)


def call(kernel, outs, ins, scratch=(), us=1.0):
    vmem = pl.BlockSpec(memory_space=pltpu.VMEM)
    scalars = pl.BlockSpec(memory_space=pltpu.SMEM)
    return pl.pallas_call(
        kernel,
        out_shape=outs,
        in_specs=[scalars if x.ndim == 1 else vmem for x in ins],
        out_specs=(vmem,) * len(outs),
        scratch_shapes=scratch,
        compiler_params=pltpu.CompilerParams(vmem_limit_bytes=16 * 2**20),
        cost_estimate=pl.CostEstimate(
            flops=int(us * 1.0e7), bytes_accessed=1 << 20, transcendentals=0
        ),
    )(*ins)


def local(doc_lengths, queries, key_rows, value_rows, grad_out):
    tokens, width = queries.shape
    dim = key_rows.shape[1]
    heads = width // dim
    rows = heads * tokens
    half = REACH // 2
    rank = lax.axis_index(AXES)
    core, chip = rank % 2, rank // 2 % 2
    place = jnp.stack([rank * tokens, core, chip]).astype(jnp.int32)

    def block(count, kind=BF16):
        return SHAPE((count, tokens, dim), kind)

    one = SHAPE((tokens, dim), BF16)
    k_four, k_eight = cyclic(key_rows, 4), cyclic(key_rows, 8)
    docs, mask, gates = call(
        docs_kernel,
        (SHAPE((REACH, tokens, 128), BF16), SHAPE((128, tokens), BF16), SHAPE((8, 128), F32)),
        (place, doc_lengths),
        us=100,
    )
    q_aug, g_t, k_own, v_own = call(
        prep_kernel,
        (SHAPE((2 * dim, rows), BF16), SHAPE((dim, rows), BF16), one, one),
        (mask, queries, grad_out, key_rows, value_rows),
        us=1,
    )

    def weigh(backs, blocks, *order):
        span = len(backs) * tokens
        return call(
            functools.partial(weigh_kernel, backs, len(blocks)),
            (SHAPE((span, rows), BF16),) + (SHAPE((heads, tokens), F32),) * 2,
            (docs, q_aug) + blocks + order,
            [pltpu.VMEM((2, span, tokens), F32)],
            us=len(backs),
        )

    v_four, v_eight = cyclic(v_own, 4), cyclic(v_own, 8)
    (k_pair,) = call(pair_kernel, (block(2),), (gates, k_own, k_four, k_eight, k_own), us=0.1)
    k_two = swapped(k_pair, 2)
    wa, ta, la = weigh((0, 4), (k_own[None], k_four[None]), k_pair, v_four, v_eight)
    (k_quad,) = call(
        quad_kernel, (block(half),), (gates, k_own, k_four, k_eight, k_two, la), us=0.1
    )
    k_odd = swapped(k_quad, 1)
    wb, tb, lb = weigh((2, 6), (k_two,), k_quad)
    (v_pair,) = call(pair_kernel, (block(2),), (gates, v_own, v_four, v_eight, k_odd), us=0.1)
    v_two = swapped(v_pair, 2)
    wc, tc, lc = weigh((1, 3, 5, 7), (k_odd,), v_pair)
    (v_quad,) = call(
        quad_kernel, (block(half),), (gates, v_own, v_four, v_eight, v_two, lc), us=0.1
    )
    v_odd = swapped(v_quad, 1)
    coef, qd_a, qd_b, qd_c, v_even, v_far = call(
        value_kernel,
        (SHAPE((3, heads, tokens), F32),) + (SHAPE((rows, dim), BF16),) * 3
        + (block(half, F32), block(half)),
        (wa, wb, wc, ta, tb, tc, la, lb, lc, queries, grad_out, v_quad),
        [pltpu.VMEM((3, rows, dim), BF16), pltpu.VMEM((128, tokens), F32)],
        us=3,
    )
    v_back = swapped(v_far, 1)
    values = (value_rows[None], v_four[None], v_two, v_odd)
    attn_out, row_dot = call(
        out_kernel,
        (SHAPE((tokens, width), BF16), SHAPE((heads, tokens), F32)),
        (wa, wb, wc, coef, g_t) + values,
        [pltpu.VMEM((dim, REACH * tokens), BF16)],
        us=3,
    )
    ds_c, k_far, v_send, v_rest = call(
        far_kernel,
        (SHAPE((half * tokens, rows), BF16), block(half), block(2), block(3, F32)),
        (gates, wc, g_t, row_dot, qd_c, v_odd, v_even, v_back),
        us=3.5,
    )
    k_back = swapped(k_far, 1)
    v_back = swapped(v_send, 2)
    ds_b, k_mid = call(
        mid_kernel,
        (SHAPE((2 * tokens, rows), BF16), block(2, F32)),
        (wb, g_t, row_dot, qd_b, v_two),
        us=1.7,
    )
    (k_send,) = call(join_kernel, (block(2),), (gates, k_mid, k_back), us=0.1)
    k_chip = swapped(k_send, 2)
    ds_a, k_near = call(
        near_kernel,
        (SHAPE((2 * tokens, rows), BF16), block(2, F32)),
        (wa, g_t, row_dot, qd_a, value_rows[None], v_four[None], k_send),
        us=1.7,
    )
    closing = (SHAPE((tokens, dim), F32), one, one)
    v_zero, v_send_four, v_send_eight = call(
        close_kernel, closing, (gates, v_rest, v_back, k_near), us=0.1
    )
    v_from_four, v_from_eight = cyclic(v_send_four, -4), cyclic(v_send_eight, -8)
    k_zero, k_send_four, k_send_eight = call(
        near_close_kernel, closing, (gates, k_near, k_back, k_chip, v_send_eight), us=0.1
    )
    k_from_four, k_from_eight = cyclic(k_send_four, -4), cyclic(k_send_eight, -8)
    (grad_queries,) = call(
        query_kernel,
        (SHAPE((tokens, width), BF16),),
        (ds_a, ds_b, ds_c, coef, key_rows[None], k_four[None], k_two, k_odd, k_send_eight),
        [pltpu.VMEM((dim, REACH * tokens), BF16)],
        us=3,
    )
    grad_values = (v_zero + v_from_four.astype(F32) + v_from_eight.astype(F32)).astype(BF16)
    grad_keys = (k_zero + k_from_four.astype(F32) + k_from_eight.astype(F32)).astype(BF16)
    return (attn_out, grad_queries, grad_keys, grad_values)


def solution(mesh):
    split = P(AXES, None)
    return jax.shard_map(
        local,
        mesh=mesh,
        in_specs=(P(), split, split, split, split),
        out_specs=(split,) * 4,
        check_vma=False,
    )
```

time: 248 us -> 69.7 us (0.28)
  the two profiles are of different devices: /device:TPU:167 before, /device:TPU:126 now
where the time goes in v2:
time: 69.7 us; the launch traced here: 69.6 us
  waiting for transfers between devices  25.3 us (36%)
  starting transfers between devices  21 us (30%)
  Pallas kernels  20.4 us (29%)
  other arithmetic  1.39 us (2%)
  between operations  0.85 us (1%)
    pallas_call x18, Pallas kernels, call(): pl.pallas_call(kernel, out_shape=outs, in_specs=[scalars if x.ndim == 1 e...  20.4 us
    ppermute x8, waiting for transfers between devices, cyclic(): lax.ppermute(value, AXES, [(s, (s + steps) % count) for s in range(count)])  20.3 us
    ppermute x8, starting transfers between devices, cyclic(): lax.ppermute(value, AXES, [(s, (s + steps) % count) for s in range(count)])  14.7 us
    ppermute x8, starting transfers between devices, swapped(): return lax.ppermute(value, AXES, [(s, s ^ bit) for s in range(count)])  6.31 us
    ppermute x8, waiting for transfers between devices, swapped(): return lax.ppermute(value, AXES, [(s, s ^ bit) for s in range(count)])  5.02 us
  transfers between devices with their start and end apart: 16, of which 8 were waited for; matrix products, arithmetic and copies ran while one was open for 1% of the time, Pallas kernels for 25%

profile of v2, /device:TPU:126, one launch (start us, length us, event | category | flops | bytes accessed | tf_op | source)
XLA Modules:
  0.0 69.6 jit_solution(6264915770279972918)
XLA Ops:
  0.7 3.2 %collective-permute-start = (bf16[256,128]{1,0:T(8,128)(2,1)}, bf16[256,128]{1,0:T(8,128)(2,1)S(1)}, u32[]{:S(2)}, u32[]{:S(2)}) collective-permute-start(bf16[256,128]{1,0:T(8,128)(2,1)} %k_ref.1), channel_id=1, source_target_pairs={{0,4},{1,5},{2,6},{3,7},{4,8},{5,9},{6,10},{7,11},{8,12},{9,13},{1... | collective-permute-start | bytes 196616 | tf_op jit(solution)/shard_map/ppermute | solution.py:21
  3.9 2.6 %collective-permute-start.1 = (bf16[256,128]{1,0:T(8,128)(2,1)}, bf16[256,128]{1,0:T(8,128)(2,1)S(1)}, u32[]{:S(2)}, u32[]{:S(2)}) collective-permute-start(bf16[256,128]{1,0:T(8,128)(2,1)} %k_ref.1), channel_id=1, source_target_pairs={{0,8},{1,9},{2,10},{3,11},{4,12},{5,13},{6,14},{7,15},{8,16},{9,17... | collective-permute-start | bytes 196616 | tf_op jit(solution)/shard_map/ppermute | solution.py:21
  6.5 0.1 pad_add_fusion.place_ref
  6.6 0.7 copy-done.4
  7.2 0.8 %shard_map.84 = (bf16[8,256,128]{2,1,0:T(8,128)(2,1)S(1)}, bf16[128,256]{1,0:T(8,128)(2,1)S(1)}, f32[8,128]{1,0:T(8,128)S(1)}) custom-call(s32[3]{0:T(128)S(1)} %pad_add_fusion.place_ref, s32[64]{0:T(128)S(1)} %copy-done.4), custom_call_target="tpu_custom_call" | custom-call | flops 1000000000 | bytes 1048576 | tf_op jit(solution)/shard_map/pallas_call | solution.py:262
  8.1 0.3 shard_map.85
  8.5 0.0 collective-permute-done.four_ref
  8.5 1.5 %collective-permute-done.1.eight_ref = bf16[256,128]{1,0:T(8,128)(2,1)S(1)} collective-permute-done((bf16[256,128]{1,0:T(8,128)(2,1)}, bf16[256,128]{1,0:T(8,128)(2,1)S(1)}, u32[]{:S(2)}, u32[]{:S(2)}) %collective-permute-start.1) | collective-permute-done | bytes 65568 | tf_op jit(solution)/shard_map/ppermute | solution.py:21
  10.0 1.0 %collective-permute-start.4 = (bf16[2,256,128]{2,1,0:T(8,128)(2,1)S(1)}, bf16[2,256,128]{2,1,0:T(8,128)(2,1)S(1)}, u32[]{:S(2)}, u32[]{:S(2)}) collective-permute-start(bf16[2,256,128]{2,1,0:T(8,128)(2,1)S(1)} %shard_map.86.refs_2_), channel_id=1, source_target_pairs={{0,2},{1,3},{2,0},{3,1},{4,6},{5,7},{6,4},{7,5},{8,10},{9,11},{10,... | collective-permute-start | bytes 393224 | tf_op jit(solution)/shard_map/ppermute | solution.py:26
  11.0 7.0 %collective-permute-start.2 = (bf16[256,128]{1,0:T(8,128)(2,1)S(1)}, bf16[256,128]{1,0:T(8,128)(2,1)S(1)}, u32[]{:S(2)}, u32[]{:S(2)}) collective-permute-start(bf16[256,128]{1,0:T(8,128)(2,1)S(1)} %get-tuple-element.47.own_ref), channel_id=1, source_target_pairs={{0,4},{1,5},{2,6},{3,7},{4,8},{5,9},{6,10},{7,11},{8,12},{9,13},{1... | collective-permute-start | bytes 196616 | tf_op jit(solution)/shard_map/ppermute | solution.py:21
  18.0 1.3 %collective-permute-start.3 = (bf16[256,128]{1,0:T(8,128)(2,1)S(1)}, bf16[256,128]{1,0:T(8,128)(2,1)S(1)}, u32[]{:S(2)}, u32[]{:S(2)}) collective-permute-start(bf16[256,128]{1,0:T(8,128)(2,1)S(1)} %get-tuple-element.47.own_ref), channel_id=1, source_target_pairs={{0,8},{1,9},{2,10},{3,11},{4,12},{5,13},{6,14},{7,15},{8,16},{9,17... | collective-permute-start | bytes 196616 | tf_op jit(solution)/shard_map/ppermute | solution.py:21
  19.3 2.2 %collective-permute-done.2.refs_3_.four_ref = bf16[256,128]{1,0:T(8,128)(2,1)S(1)} collective-permute-done((bf16[256,128]{1,0:T(8,128)(2,1)S(1)}, bf16[256,128]{1,0:T(8,128)(2,1)S(1)}, u32[]{:S(2)}, u32[]{:S(2)}) %collective-permute-start.2) | collective-permute-done | bytes 65568 | tf_op jit(solution)/shard_map/ppermute | solution.py:21
  21.5 2.3 %collective-permute-done.3.refs_4_.eight_ref = bf16[256,128]{1,0:T(8,128)(2,1)S(1)} collective-permute-done((bf16[256,128]{1,0:T(8,128)(2,1)S(1)}, bf16[256,128]{1,0:T(8,128)(2,1)S(1)}, u32[]{:S(2)}, u32[]{:S(2)}) %collective-permute-start.3) | collective-permute-done | bytes 65568 | tf_op jit(solution)/shard_map/ppermute | solution.py:21
  23.7 1.4 %shard_map.87 = (bf16[512,2048]{1,0:T(8,128)(2,1)S(1)}, f32[8,256]{1,0:T(8,128)S(1)}, f32[8,256]{1,0:T(8,128)S(1)}) custom-call(bf16[8,256,128]{2,1,0:T(8,128)(2,1)S(1)} %get-tuple-element.42.docs_ref, bf16[256,2048]{1,0:T(8,128)(2,1)S(1)} %get-tuple-element.44.qa_ref, bf16[1,256,128]{2,1,0:T(8,128)(2,1)S(1)} %bitcast.12, bf16[1,256,128]{2,1,0:T(8,128)(2,1)S(1)} %bitcast.10, ...), custom_call_target="tpu_custom_call" | custom-call | flops 20000000 | bytes 1048576 | tf_op jit(solution)/shard_map/pallas_call | solution.py:262
  25.2 0.0 collective-permute-done.4.two_ref.refs_0_
  25.2 0.1 shard_map.88.refs_1_
  25.2 0.1 collective-permute-start.5
  25.3 1.5 %collective-permute-done.5.order_ref.refs_0_.odd_ref = bf16[4,256,128]{2,1,0:T(8,128)(2,1)S(1)} collective-permute-done((bf16[4,256,128]{2,1,0:T(8,128)(2,1)S(1)}, bf16[4,256,128]{2,1,0:T(8,128)(2,1)S(1)}, u32[]{:S(2)}, u32[]{:S(2)}) %collective-permute-start.5) | collective-permute-done | bytes 262176 | tf_op jit(solution)/shard_map/ppermute | solution.py:26
  26.9 2.0 %collective-permute-start.6 = (bf16[2,256,128]{2,1,0:T(8,128)(2,1)S(1)}, bf16[2,256,128]{2,1,0:T(8,128)(2,1)S(1)}, u32[]{:S(2)}, u32[]{:S(2)}) collective-permute-start(bf16[2,256,128]{2,1,0:T(8,128)(2,1)S(1)} %shard_map.90.refs_1_), channel_id=1, source_target_pairs={{0,2},{1,3},{2,0},{3,1},{4,6},{5,7},{6,4},{7,5},{8,10},{9,11},{10,... | collective-permute-start | bytes 393224 | tf_op jit(solution)/shard_map/ppermute | solution.py:26
  28.9 1.6 %shard_map.89 = (bf16[512,2048]{1,0:T(8,128)(2,1)S(1)}, f32[8,256]{1,0:T(8,128)S(1)}, f32[8,256]{1,0:T(8,128)S(1)}) custom-call(bf16[8,256,128]{2,1,0:T(8,128)(2,1)S(1)} %get-tuple-element.42.docs_ref, bf16[256,2048]{1,0:T(8,128)(2,1)S(1)} %get-tuple-element.44.qa_ref, bf16[2,256,128]{2,1,0:T(8,128)(2,1)S(1)} %collective-permute-done.4.two_ref.refs_0_, ...), custom_call_target="tpu_custom_call" | custom-call | flops 20000000 | bytes 1048576 | tf_op jit(solution)/shard_map/pallas_call | solution.py:262
  30.5 3.1 %shard_map.91 = (bf16[1024,2048]{1,0:T(8,128)(2,1)S(1)}, f32[8,256]{1,0:T(8,128)S(1)}, f32[8,256]{1,0:T(8,128)S(1)}) custom-call(bf16[8,256,128]{2,1,0:T(8,128)(2,1)S(1)} %get-tuple-element.42.docs_ref, bf16[256,2048]{1,0:T(8,128)(2,1)S(1)} %get-tuple-element.44.qa_ref, bf16[4,256,128]{2,1,0:T(8,128)(2,1)S(1)} %collective-permute-done.5.order_ref.refs_0_.odd_ref, ...), custom_call_target="tpu_custom_call" | custom-call | flops 40000000 | bytes 1048576 | tf_op jit(solution)/shard_map/pallas_call | solution.py:262
  33.6 0.0 collective-permute-done.6.two_ref
  33.6 0.1 shard_map.92.order_ref
  33.7 0.3 collective-permute-start.7
  33.9 2.9 %shard_map.93 = (f32[3,8,256]{2,1,0:T(8,128)S(1)}, bf16[2048,128]{1,0:T(8,128)(2,1)S(1)}, bf16[2048,128]{1,0:T(8,128)(2,1)S(1)}, bf16[2048,128]{1,0:T(8,128)(2,1...) custom-call(bf16[512,2048]{1,0:T(8,128)(2,1)S(1)} %get-tuple-element.48.wa_ref.w_ref, ...), custom_call_target="tpu_custom_call" | custom-call | flops 30000000 | bytes 1048576 | tf_op jit(solution)/shard_map/pallas_call | solution.py:262
  36.9 0.6 collective-permute-start.8
  37.5 2.5 %shard_map.94 = (bf16[256,1024]{1,0:T(8,128)(2,1)}, f32[8,256]{1,0:T(8,128)S(1)}) custom-call(bf16[512,2048]{1,0:T(8,128)(2,1)S(1)} %get-tuple-element.48.wa_ref.w_ref, bf16[512,2048]{1,0:T(8,128)(2,1)S(1)} %get-tuple-element.50.wb_ref.w_ref, bf16[1024,2048]{1,0:T(8,128)(2,1)S(1)} %get-tuple-element.51.wc_ref.w_ref, ...), custom_call_target="tpu_custom_call" | custom-call | flops 30000000 | bytes 1048576 | tf_op jit(solution)/shard_map/pallas_call | solution.py:262
  39.9 0.0 collective-permute-done.8.back_ref
  39.9 2.5 %shard_map.96 = (bf16[1024,2048]{1,0:T(8,128)(2,1)S(1)}, bf16[4,256,128]{2,1,0:T(8,128)(2,1)S(1)}, bf16[2,256,128]{2,1,0:T(8,128)(2,1)S(1)}, f32[3,256,128]{2,1,0:T(8,128)S(1)}) custom-call(f32[8,128]{1,0:T(8,128)S(1)} %get-tuple-element.46.gates_ref, bf16[1024,2048]{1,0:T(8,128)(2,1)S(1)} %get-tuple-element.51.wc_ref.w_ref, ...), custom_call_target="tpu_custom_call" | custom-call | flops 35000000 | bytes 1048576 | tf_op jit(solution)/shard_map/pallas_call | solution.py:262
  42.4 0.1 collective-permute-start.9
  42.5 0.9 %collective-permute-start.11 = (bf16[2,256,128]{2,1,0:T(8,128)(2,1)S(1)}, bf16[2,256,128]{2,1,0:T(8,128)(2,1)S(1)}, u32[]{:S(2)}, u32[]{:S(2)}) collective-permute-start(bf16[2,256,128]{2,1,0:T(8,128)(2,1)S(1)} %get-tuple-element.73), channel_id=1, source_target_pairs={{0,2},{1,3},{2,0},{3,1},{4,6},{5,7},{6,4},{7,5},{8,10},{9,11},{10,... | collective-permute-start | bytes 393224 | tf_op jit(solution)/shard_map/ppermute | solution.py:26
  43.5 1.3 %shard_map.95 = (bf16[512,2048]{1,0:T(8,128)(2,1)S(1)}, f32[2,256,128]{2,1,0:T(8,128)S(1)}) custom-call(bf16[512,2048]{1,0:T(8,128)(2,1)S(1)} %get-tuple-element.50.wb_ref.w_ref, bf16[128,2048]{1,0:T(8,128)(2,1)S(1)} %get-tuple-element.58.gt_ref, f32[8,256]{1,0:T(8,128)S(1)} %get-tuple-element.60.dot_ref, bf16[2048,128]{1,0:T(8,128)(2,1)S(1)} %get-tuple-element.62.qd_ref, ...), custom_call_target="tpu_custom_call" | custom-call | flops 17000000 | bytes 1048576 | tf_op jit(solution)/shard_map/pallas_call | solution.py:262
  44.8 1.2 %collective-permute-start.10 = (bf16[2,256,128]{2,1,0:T(8,128)(2,1)S(1)}, bf16[2,256,128]{2,1,0:T(8,128)(2,1)S(1)}, u32[]{:S(2)}, u32[]{:S(2)}) collective-permute-start(bf16[2,256,128]{2,1,0:T(8,128)(2,1)S(1)} %shard_map.97.order_ref), channel_id=1, source_target_pairs={{0,2},{1,3},{2,0},{3,1},{4,6},{5,7},{6,4},{7,5},{8,10},{9,11},{10,... | collective-permute-start | bytes 393224 | tf_op jit(solution)/shard_map/ppermute | solution.py:26
  46.0 1.3 %shard_map.98 = (bf16[512,2048]{1,0:T(8,128)(2,1)S(1)}, f32[2,256,128]{2,1,0:T(8,128)S(1)}) custom-call(bf16[512,2048]{1,0:T(8,128)(2,1)S(1)} %get-tuple-element.48.wa_ref.w_ref, bf16[128,2048]{1,0:T(8,128)(2,1)S(1)} %get-tuple-element.58.gt_ref, f32[8,256]{1,0:T(8,128)S(1)} %get-tuple-element.60.dot_ref, bf16[2048,128]{1,0:T(8,128)(2,1)S(1)} %get-tuple-element.61.qd_ref, ...), custom_call_target="tpu_custom_call" | custom-call | flops 17000000 | bytes 1048576 | tf_op jit(solution)/shard_map/pallas_call | solution.py:262
  47.3 1.6 %collective-permute-done.11.back_ref = bf16[2,256,128]{2,1,0:T(8,128)(2,1)S(1)} collective-permute-done((bf16[2,256,128]{2,1,0:T(8,128)(2,1)S(1)}, bf16[2,256,128]{2,1,0:T(8,128)(2,1)S(1)}, u32[]{:S(2)}, u32[]{:S(2)}) %collective-permute-start.11) | collective-permute-done | bytes 131104 | tf_op jit(solution)/shard_map/ppermute | solution.py:26
  49.0 0.1 collective-permute-start.15
  49.0 0.3 collective-permute-start.14
  49.4 1.9 %collective-permute-done.10.chip_ref = bf16[2,256,128]{2,1,0:T(8,128)(2,1)S(1)} collective-permute-done((bf16[2,256,128]{2,1,0:T(8,128)(2,1)S(1)}, bf16[2,256,128]{2,1,0:T(8,128)(2,1)S(1)}, u32[]{:S(2)}, u32[]{:S(2)}) %collective-permute-start.10) | collective-permute-done | bytes 131104 | tf_op jit(solution)/shard_map/ppermute | solution.py:26
  51.2 0.1 shard_map.100
  51.3 0.1 collective-permute-start.13
  51.4 0.1 collective-permute-start.12
  51.5 11.2 %collective-permute-done.15 = bf16[256,128]{1,0:T(8,128)(2,1)S(1)} collective-permute-done((bf16[256,128]{1,0:T(8,128)(2,1)S(1)}, bf16[256,128]{1,0:T(8,128)(2,1)S(1)}, u32[]{:S(2)}, u32[]{:S(2)}) %collective-permute-start.15) | collective-permute-done | bytes 65568 | tf_op jit(solution)/shard_map/ppermute | solution.py:21
  62.7 3.2 %collective-permute-done.14 = bf16[256,128]{1,0:T(8,128)(2,1)S(1)} collective-permute-done((bf16[256,128]{1,0:T(8,128)(2,1)S(1)}, bf16[256,128]{1,0:T(8,128)(2,1)S(1)}, u32[]{:S(2)}, u32[]{:S(2)}) %collective-permute-start.14) | collective-permute-done | bytes 65568 | tf_op jit(solution)/shard_map/ppermute | solution.py:21
  65.9 0.7 add_convert_fusion
  66.6 2.3 %shard_map.101 = bf16[256,1024]{1,0:T(8,128)(2,1)} custom-call(bf16[512,2048]{1,0:T(8,128)(2,1)S(1)} %get-tuple-element.68.da_ref, bf16[512,2048]{1,0:T(8,128)(2,1)S(1)} %get-tuple-element.69.db_ref, bf16[1024,2048]{1,0:T(8,128)(2,1)S(1)} %get-tuple-element.70.dc_ref, f32[3,8,256]{2,1,0:T(8,128)S(1)} %get-tuple-element.57.coef_ref, ...), custom_call_target="tpu_custom_call" | custom-call | flops 30000000 | bytes 1048576 | tf_op jit(solution)/shard_map/pallas_call | solution.py:262
  68.9 0.0 collective-permute-done.13
  68.9 0.0 collective-permute-done.12
  68.9 0.7 add_convert_fusion.1
  (15 shorter events, 0.2 us)
Async XLA Ops:
  0.6 7.5 %copy-start.3 = (bf16[256,128]{1,0:T(8,128)(2,1)S(1)}, bf16[256,128]{1,0:T(8,128)(2,1)}, u32[]{:S(2)}) copy-start(bf16[256,128]{1,0:T(8,128)(2,1)} %k_ref.1) | copy-start | bytes 196612
  0.6 7.5 %copy-start = (bf16[256,1024]{1,0:T(8,128)(2,1)S(1)}, bf16[256,1024]{1,0:T(8,128)(2,1)}, u32[]{:S(2)}) copy-start(bf16[256,1024]{1,0:T(8,128)(2,1)} %q_ref.3) | copy-start | bytes 1572868
  0.7 7.5 %copy-start.1 = (bf16[256,1024]{1,0:T(8,128)(2,1)S(1)}, bf16[256,1024]{1,0:T(8,128)(2,1)}, u32[]{:S(2)}) copy-start(bf16[256,1024]{1,0:T(8,128)(2,1)} %g_ref.3) | copy-start | bytes 1572868
  0.7 7.5 %copy-start.2 = (bf16[256,128]{1,0:T(8,128)(2,1)S(1)}, bf16[256,128]{1,0:T(8,128)(2,1)}, u32[]{:S(2)}) copy-start(bf16[256,128]{1,0:T(8,128)(2,1)} %v_ref.1) | copy-start | bytes 196612
  0.7 7.8 %collective-permute-start = (bf16[256,128]{1,0:T(8,128)(2,1)}, bf16[256,128]{1,0:T(8,128)(2,1)S(1)}, u32[]{:S(2)}, u32[]{:S(2)}) collective-permute-start(bf16[256,128]{1,0:T(8,128)(2,1)} %k_ref.1), channel_id=1, source_target_pairs={{0,4},{1,5},{2,6},{3,7},{4,8},{5,9},{6,10},{7,11},{8,12},{9,13},{1... | collective-permute-start | bytes 196616 | tf_op jit(solution)/shard_map/ppermute | solution.py:21
  3.9 6.0 %collective-permute-start.1 = (bf16[256,128]{1,0:T(8,128)(2,1)}, bf16[256,128]{1,0:T(8,128)(2,1)S(1)}, u32[]{:S(2)}, u32[]{:S(2)}) collective-permute-start(bf16[256,128]{1,0:T(8,128)(2,1)} %k_ref.1), channel_id=1, source_target_pairs={{0,8},{1,9},{2,10},{3,11},{4,12},{5,13},{6,14},{7,15},{8,16},{9,17... | collective-permute-start | bytes 196616 | tf_op jit(solution)/shard_map/ppermute | solution.py:21
  6.6 0.7 copy-start.4
  10.0 15.2 %collective-permute-start.4 = (bf16[2,256,128]{2,1,0:T(8,128)(2,1)S(1)}, bf16[2,256,128]{2,1,0:T(8,128)(2,1)S(1)}, u32[]{:S(2)}, u32[]{:S(2)}) collective-permute-start(bf16[2,256,128]{2,1,0:T(8,128)(2,1)S(1)} %shard_map.86.refs_2_), channel_id=1, source_target_pairs={{0,2},{1,3},{2,0},{3,1},{4,6},{5,7},{6,4},{7,5},{8,10},{9,11},{10,... | collective-permute-start | bytes 393224 | tf_op jit(solution)/shard_map/ppermute | solution.py:26
  11.0 10.5 %collective-permute-start.2 = (bf16[256,128]{1,0:T(8,128)(2,1)S(1)}, bf16[256,128]{1,0:T(8,128)(2,1)S(1)}, u32[]{:S(2)}, u32[]{:S(2)}) collective-permute-start(bf16[256,128]{1,0:T(8,128)(2,1)S(1)} %get-tuple-element.47.own_ref), channel_id=1, source_target_pairs={{0,4},{1,5},{2,6},{3,7},{4,8},{5,9},{6,10},{7,11},{8,12},{9,13},{1... | collective-permute-start | bytes 196616 | tf_op jit(solution)/shard_map/ppermute | solution.py:21
  18.0 5.8 %collective-permute-start.3 = (bf16[256,128]{1,0:T(8,128)(2,1)S(1)}, bf16[256,128]{1,0:T(8,128)(2,1)S(1)}, u32[]{:S(2)}, u32[]{:S(2)}) collective-permute-start(bf16[256,128]{1,0:T(8,128)(2,1)S(1)} %get-tuple-element.47.own_ref), channel_id=1, source_target_pairs={{0,8},{1,9},{2,10},{3,11},{4,12},{5,13},{6,14},{7,15},{8,16},{9,17... | collective-permute-start | bytes 196616 | tf_op jit(solution)/shard_map/ppermute | solution.py:21
  25.2 1.6 %collective-permute-start.5 = (bf16[4,256,128]{2,1,0:T(8,128)(2,1)S(1)}, bf16[4,256,128]{2,1,0:T(8,128)(2,1)S(1)}, u32[]{:S(2)}, u32[]{:S(2)}) collective-permute-start(bf16[4,256,128]{2,1,0:T(8,128)(2,1)S(1)} %shard_map.88.refs_1_), channel_id=1, source_target_pairs={{0,1},{1,0},{2,3},{3,2},{4,5},{5,4},{6,7},{7,6},{8,9},{9,8},{10,11... | collective-permute-start | bytes 786440 | tf_op jit(solution)/shard_map/ppermute | solution.py:26
  26.9 6.7 %collective-permute-start.6 = (bf16[2,256,128]{2,1,0:T(8,128)(2,1)S(1)}, bf16[2,256,128]{2,1,0:T(8,128)(2,1)S(1)}, u32[]{:S(2)}, u32[]{:S(2)}) collective-permute-start(bf16[2,256,128]{2,1,0:T(8,128)(2,1)S(1)} %shard_map.90.refs_1_), channel_id=1, source_target_pairs={{0,2},{1,3},{2,0},{3,1},{4,6},{5,7},{6,4},{7,5},{8,10},{9,11},{10,... | collective-permute-start | bytes 393224 | tf_op jit(solution)/shard_map/ppermute | solution.py:26
  33.7 3.8 %collective-permute-start.7 = (bf16[4,256,128]{2,1,0:T(8,128)(2,1)S(1)}, bf16[4,256,128]{2,1,0:T(8,128)(2,1)S(1)}, u32[]{:S(2)}, u32[]{:S(2)}) collective-permute-start(bf16[4,256,128]{2,1,0:T(8,128)(2,1)S(1)} %shard_map.92.order_ref), channel_id=1, source_target_pairs={{0,1},{1,0},{2,3},{3,2},{4,5},{5,4},{6,7},{7,6},{8,9},{9,8},{10,11... | collective-permute-start | bytes 786440 | tf_op jit(solution)/shard_map/ppermute | solution.py:26
  36.9 3.0 %collective-permute-start.8 = (bf16[4,256,128]{2,1,0:T(8,128)(2,1)S(1)}, bf16[4,256,128]{2,1,0:T(8,128)(2,1)S(1)}, u32[]{:S(2)}, u32[]{:S(2)}) collective-permute-start(bf16[4,256,128]{2,1,0:T(8,128)(2,1)S(1)} %get-tuple-element.66), channel_id=1, source_target_pairs={{0,1},{1,0},{2,3},{3,2},{4,5},{5,4},{6,7},{7,6},{8,9},{9,8},{10,11... | collective-permute-start | bytes 786440 | tf_op jit(solution)/shard_map/ppermute | solution.py:26
  42.4 2.3 %collective-permute-start.9 = (bf16[4,256,128]{2,1,0:T(8,128)(2,1)S(1)}, bf16[4,256,128]{2,1,0:T(8,128)(2,1)S(1)}, u32[]{:S(2)}, u32[]{:S(2)}) collective-permute-start(bf16[4,256,128]{2,1,0:T(8,128)(2,1)S(1)} %get-tuple-element.67), channel_id=1, source_target_pairs={{0,1},{1,0},{2,3},{3,2},{4,5},{5,4},{6,7},{7,6},{8,9},{9,8},{10,11... | collective-permute-start | bytes 786440 | tf_op jit(solution)/shard_map/ppermute | solution.py:26
  42.5 6.4 %collective-permute-start.11 = (bf16[2,256,128]{2,1,0:T(8,128)(2,1)S(1)}, bf16[2,256,128]{2,1,0:T(8,128)(2,1)S(1)}, u32[]{:S(2)}, u32[]{:S(2)}) collective-permute-start(bf16[2,256,128]{2,1,0:T(8,128)(2,1)S(1)} %get-tuple-element.73), channel_id=1, source_target_pairs={{0,2},{1,3},{2,0},{3,1},{4,6},{5,7},{6,4},{7,5},{8,10},{9,11},{10,... | collective-permute-start | bytes 393224 | tf_op jit(solution)/shard_map/ppermute | solution.py:26
  44.8 6.4 %collective-permute-start.10 = (bf16[2,256,128]{2,1,0:T(8,128)(2,1)S(1)}, bf16[2,256,128]{2,1,0:T(8,128)(2,1)S(1)}, u32[]{:S(2)}, u32[]{:S(2)}) collective-permute-start(bf16[2,256,128]{2,1,0:T(8,128)(2,1)S(1)} %shard_map.97.order_ref), channel_id=1, source_target_pairs={{0,2},{1,3},{2,0},{3,1},{4,6},{5,7},{6,4},{7,5},{8,10},{9,11},{10,... | collective-permute-start | bytes 393224 | tf_op jit(solution)/shard_map/ppermute | solution.py:26
  49.0 13.7 %collective-permute-start.15 = (bf16[256,128]{1,0:T(8,128)(2,1)S(1)}, bf16[256,128]{1,0:T(8,128)(2,1)S(1)}, u32[]{:S(2)}, u32[]{:S(2)}) collective-permute-start(bf16[256,128]{1,0:T(8,128)(2,1)S(1)} %get-tuple-element.74.order_ref), channel_id=1, source_target_pairs={{0,248},{1,249},{2,250},{3,251},{4,252},{5,253},{6,254},{7,255},{8... | collective-permute-start | bytes 196616 | tf_op jit(solution)/shard_map/ppermute | solution.py:21
  49.0 16.9 %collective-permute-start.14 = (bf16[256,128]{1,0:T(8,128)(2,1)S(1)}, bf16[256,128]{1,0:T(8,128)(2,1)S(1)}, u32[]{:S(2)}, u32[]{:S(2)}) collective-permute-start(bf16[256,128]{1,0:T(8,128)(2,1)S(1)} %get-tuple-element.79), channel_id=1, source_target_pairs={{0,252},{1,253},{2,254},{3,255},{4,0},{5,1},{6,2},{7,3},{8,4},{9,5... | collective-permute-start | bytes 196616 | tf_op jit(solution)/shard_map/ppermute | solution.py:21
  51.3 17.6 %collective-permute-start.13 = (bf16[256,128]{1,0:T(8,128)(2,1)S(1)}, bf16[256,128]{1,0:T(8,128)(2,1)S(1)}, u32[]{:S(2)}, u32[]{:S(2)}) collective-permute-start(bf16[256,128]{1,0:T(8,128)(2,1)S(1)} %get-tuple-element.75.order_ref), channel_id=1, source_target_pairs={{0,248},{1,249},{2,250},{3,251},{4,252},{5,253},{6,254},{7,255},{8... | collective-permute-start | bytes 196616 | tf_op jit(solution)/shard_map/ppermute | solution.py:21
  51.4 17.5 %collective-permute-start.12 = (bf16[256,128]{1,0:T(8,128)(2,1)S(1)}, bf16[256,128]{1,0:T(8,128)(2,1)S(1)}, u32[]{:S(2)}, u32[]{:S(2)}) collective-permute-start(bf16[256,128]{1,0:T(8,128)(2,1)S(1)} %get-tuple-element.77), channel_id=1, source_target_pairs={{0,252},{1,253},{2,254},{3,255},{4,0},{5,1},{6,2},{7,3},{8,4},{9,5... | collective-permute-start | bytes 196616 | tf_op jit(solution)/shard_map/ppermute | solution.py:21

commit v3 on v2

--- a/solution.py
+++ b/solution.py
@@ -18,7 +18,10 @@
 
 def cyclic(value, steps):
     count = lax.axis_size(AXES)
-    return lax.ppermute(value, AXES, [(s, (s + steps) % count) for s in range(count)])
+    pairs = [(s, (s + steps) % count) for s in range(count)]
+    if abs(steps) == 8:
+        pairs = [p for p in pairs if p[0] % 4]
+    return lax.ppermute(value, AXES, pairs)
 
 
 def swapped(value, bit):
@@ -197,7 +200,8 @@
     )
 
 
-def pair_kernel(gates_ref, own_ref, four_ref, eight_ref, order_ref, send_ref):
+def pair_kernel(gates_ref, own_ref, four_ref, eight_ref, *refs):
+    send_ref = refs[-1]
     upper = gates_ref[1:2, :] > 0
     send_ref[0] = jnp.where(upper, four_ref[...].astype(F32), own_ref[...].astype(F32)).astype(BF16)
     send_ref[1] = jnp.where(upper, eight_ref[...].astype(F32), four_ref[...].astype(F32)).astype(BF16)
@@ -286,7 +290,9 @@
         return SHAPE((count, tokens, dim), kind)
 
     one = SHAPE((tokens, dim), BF16)
-    k_four, k_eight = cyclic(key_rows, 4), cyclic(key_rows, 8)
+    both = jnp.stack([key_rows, value_rows])
+    four, eight = cyclic(both, 4), cyclic(both, 8)
+    (k_four, v_four), (k_eight, v_eight) = four, eight
     docs, mask, gates = call(
         docs_kernel,
         (SHAPE((REACH, tokens, 128), BF16), SHAPE((128, tokens), BF16), SHAPE((8, 128), F32)),
@@ -310,16 +316,15 @@
             us=len(backs),
         )
 
-    v_four, v_eight = cyclic(v_own, 4), cyclic(v_own, 8)
-    (k_pair,) = call(pair_kernel, (block(2),), (gates, k_own, k_four, k_eight, k_own), us=0.1)
+    (k_pair,) = call(pair_kernel, (block(2),), (gates, k_own, k_four, k_eight), us=0.1)
     k_two = swapped(k_pair, 2)
-    wa, ta, la = weigh((0, 4), (k_own[None], k_four[None]), k_pair, v_four, v_eight)
+    wa, ta, la = weigh((0, 4), (k_own[None], k_four[None]), k_pair)
     (k_quad,) = call(
         quad_kernel, (block(half),), (gates, k_own, k_four, k_eight, k_two, la), us=0.1
     )
     k_odd = swapped(k_quad, 1)
     wb, tb, lb = weigh((2, 6), (k_two,), k_quad)
-    (v_pair,) = call(pair_kernel, (block(2),), (gates, v_own, v_four, v_eight, k_odd), us=0.1)
+    (v_pair,) = call(pair_kernel, (block(2),), (gates, v_own, v_four, v_eight, k_quad), us=0.1)
     v_two = swapped(v_pair, 2)
     wc, tc, lc = weigh((1, 3, 5, 7), (k_odd,), v_pair)
     (v_quad,) = call(

time: 69.7 us -> 63.3 us (0.908)
  the two profiles are of different devices: /device:TPU:126 before, /device:TPU:34 now
where the time goes in v3:
time: 63.3 us; the launch traced here: 63.2 us
  starting transfers between devices  27.8 us (44%)
  Pallas kernels  20.4 us (32%)
  waiting for transfers between devices  11 us (17%)
  other arithmetic  2.37 us (4%)
  between operations  0.9 us (1%)
  local copies, waits for them, and re-layouts  0.72 us (1%)
    ppermute x6, starting transfers between devices, cyclic(): return lax.ppermute(value, AXES, pairs)  24.3 us
    pallas_call x18, Pallas kernels, call(): pl.pallas_call(kernel, out_shape=outs, in_specs=[scalars if x.ndim == 1 e...  20.4 us
    ppermute x8, waiting for transfers between devices, swapped(): return lax.ppermute(value, AXES, [(s, s ^ bit) for s in range(count)])  6.3 us
    ppermute x6, waiting for transfers between devices, cyclic(): return lax.ppermute(value, AXES, pairs)  4.69 us
    ppermute x8, starting transfers between devices, swapped(): return lax.ppermute(value, AXES, [(s, s ^ bit) for s in range(count)])  3.43 us
  transfers between devices with their start and end apart: 14, of which 5 were waited for; matrix products, arithmetic and copies ran while one was open for 1% of the time, Pallas kernels for 28%

profile of v3, /device:TPU:34, one launch (start us, length us, event | category | flops | bytes accessed | tf_op | source)
XLA Modules:
  0.0 63.2 jit_solution(470609332570955253)
XLA Ops:
  0.7 1.0 %pad_maximum_fusion = bf16[2,256,128]{2,1,0:T(8,128)(2,1)S(1)} fusion(bf16[1,256,128]{2,1,0:T(8,128)(2,1)} %bitcast.14, bf16[1,256,128]{2,1,0:T(8,128)(2,1)} %bitcast.17), kind=kLoop, calls=%fused_computation | loop fusion | flops 65536 | bytes 262144 | tf_op jit(solution)/shard_map/stack | solution.py:293
  1.7 1.7 %collective-permute-start = (bf16[2,256,128]{2,1,0:T(8,128)(2,1)S(1)}, bf16[2,256,128]{2,1,0:T(8,128)(2,1)S(1)}, u32[]{:S(2)}, u32[]{:S(2)}) collective-permute-start(bf16[2,256,128]{2,1,0:T(8,128)(2,1)S(1)} %pad_maximum_fusion), channel_id=1, source_target_pairs={{0,4},{1,5},{2,6},{3,7},{4,8},{5,9},{6,10},{7,11},{8,12},{9,13},{1... | collective-permute-start | bytes 393224 | tf_op jit(solution)/shard_map/ppermute | solution.py:24
  3.3 4.8 %collective-permute-start.1 = (bf16[2,256,128]{2,1,0:T(8,128)(2,1)S(1)}, bf16[2,256,128]{2,1,0:T(8,128)(2,1)S(1)}, u32[]{:S(2)}, u32[]{:S(2)}) collective-permute-start(bf16[2,256,128]{2,1,0:T(8,128)(2,1)S(1)} %pad_maximum_fusion), channel_id=1, source_target_pairs={{1,9},{2,10},{3,11},{5,13},{6,14},{7,15},{9,17},{10,18},{11,19},{1... | collective-permute-start | bytes 393224 | tf_op jit(solution)/shard_map/ppermute | solution.py:24
  8.1 0.1 pad_add_fusion.place_ref
  8.2 0.7 %copy-done.4 = s32[64]{0:T(128)S(1)} copy-done((s32[64]{0:T(128)S(1)}, s32[64]{0:T(128)}, u32[]{:S(2)}) %copy-start.4) | copy-done | bytes 280
  8.9 0.8 %shard_map.84 = (bf16[8,256,128]{2,1,0:T(8,128)(2,1)S(1)}, bf16[128,256]{1,0:T(8,128)(2,1)S(1)}, f32[8,128]{1,0:T(8,128)S(1)}) custom-call(s32[3]{0:T(128)S(1)} %pad_add_fusion.place_ref, s32[64]{0:T(128)S(1)} %copy-done.4), custom_call_target="tpu_custom_call" | custom-call | flops 1000000000 | bytes 1048576 | tf_op jit(solution)/shard_map/pallas_call | solution.py:266
  9.8 0.3 shard_map.85
  10.1 0.0 collective-permute-done
  10.2 2.4 %collective-permute-done.1 = bf16[2,256,128]{2,1,0:T(8,128)(2,1)S(1)} collective-permute-done((bf16[2,256,128]{2,1,0:T(8,128)(2,1)S(1)}, bf16[2,256,128]{2,1,0:T(8,128)(2,1)S(1)}, u32[]{:S(2)}, u32[]{:S(2)}) %collective-permute-start.1) | collective-permute-done | bytes 131104 | tf_op jit(solution)/shard_map/ppermute | solution.py:24
  12.6 0.1 collective-permute-start.2
  12.7 1.4 %shard_map.87 = (bf16[512,2048]{1,0:T(8,128)(2,1)S(1)}, f32[8,256]{1,0:T(8,128)S(1)}, f32[8,256]{1,0:T(8,128)S(1)}) custom-call(bf16[8,256,128]{2,1,0:T(8,128)(2,1)S(1)} %get-tuple-element.42.docs_ref, bf16[256,2048]{1,0:T(8,128)(2,1)S(1)} %get-tuple-element.44.qa_ref, bf16[1,256,128]{2,1,0:T(8,128)(2,1)S(1)} %bitcast.19, ...), custom_call_target="tpu_custom_call" | custom-call | flops 20000000 | bytes 1048576 | tf_op jit(solution)/shard_map/pallas_call | solution.py:266
  14.1 3.5 %collective-permute-done.2.two_ref.refs_0_ = bf16[2,256,128]{2,1,0:T(8,128)(2,1)S(1)} collective-permute-done((bf16[2,256,128]{2,1,0:T(8,128)(2,1)S(1)}, bf16[2,256,128]{2,1,0:T(8,128)(2,1)S(1)}, u32[]{:S(2)}, u32[]{:S(2)}) %collective-permute-start.2) | collective-permute-done | bytes 131104 | tf_op jit(solution)/shard_map/ppermute | solution.py:29
  17.7 0.1 shard_map.88.refs_1_.refs_0_
  17.7 0.1 collective-permute-start.3
  17.9 0.1 collective-permute-start.4
  18.0 1.6 %shard_map.89 = (bf16[512,2048]{1,0:T(8,128)(2,1)S(1)}, f32[8,256]{1,0:T(8,128)S(1)}, f32[8,256]{1,0:T(8,128)S(1)}) custom-call(bf16[8,256,128]{2,1,0:T(8,128)(2,1)S(1)} %get-tuple-element.42.docs_ref, bf16[256,2048]{1,0:T(8,128)(2,1)S(1)} %get-tuple-element.44.qa_ref, bf16[2,256,128]{2,1,0:T(8,128)(2,1)S(1)} %collective-permute-done.2.two_ref.refs_0_, ...), custom_call_target="tpu_custom_call" | custom-call | flops 20000000 | bytes 1048576 | tf_op jit(solution)/shard_map/pallas_call | solution.py:266
  19.6 0.0 collective-permute-done.3.refs_0_.odd_ref
  19.6 3.1 %shard_map.91 = (bf16[1024,2048]{1,0:T(8,128)(2,1)S(1)}, f32[8,256]{1,0:T(8,128)S(1)}, f32[8,256]{1,0:T(8,128)S(1)}) custom-call(bf16[8,256,128]{2,1,0:T(8,128)(2,1)S(1)} %get-tuple-element.42.docs_ref, bf16[256,2048]{1,0:T(8,128)(2,1)S(1)} %get-tuple-element.44.qa_ref, bf16[4,256,128]{2,1,0:T(8,128)(2,1)S(1)} %collective-permute-done.3.refs_0_.odd_ref, ...), custom_call_target="tpu_custom_call" | custom-call | flops 40000000 | bytes 1048576 | tf_op jit(solution)/shard_map/pallas_call | solution.py:266
  22.7 1.2 %collective-permute-done.4.two_ref = bf16[2,256,128]{2,1,0:T(8,128)(2,1)S(1)} collective-permute-done((bf16[2,256,128]{2,1,0:T(8,128)(2,1)S(1)}, bf16[2,256,128]{2,1,0:T(8,128)(2,1)S(1)}, u32[]{:S(2)}, u32[]{:S(2)}) %collective-permute-start.4) | collective-permute-done | bytes 131104 | tf_op jit(solution)/shard_map/ppermute | solution.py:29
  23.8 0.1 shard_map.92.order_ref
  23.9 0.3 collective-permute-start.5
  24.2 2.9 %shard_map.93 = (f32[3,8,256]{2,1,0:T(8,128)S(1)}, bf16[2048,128]{1,0:T(8,128)(2,1)S(1)}, bf16[2048,128]{1,0:T(8,128)(2,1)S(1)}, bf16[2048,128]{1,0:T(8,128)(2,1...) custom-call(bf16[512,2048]{1,0:T(8,128)(2,1)S(1)} %get-tuple-element.47.wa_ref.w_ref, ...), custom_call_target="tpu_custom_call" | custom-call | flops 30000000 | bytes 1048576 | tf_op jit(solution)/shard_map/pallas_call | solution.py:266
  27.1 0.6 collective-permute-start.6
  27.7 0.0 collective-permute-done.5.odd_ref
  27.7 2.4 %shard_map.94 = (bf16[256,1024]{1,0:T(8,128)(2,1)}, f32[8,256]{1,0:T(8,128)S(1)}) custom-call(bf16[512,2048]{1,0:T(8,128)(2,1)S(1)} %get-tuple-element.47.wa_ref.w_ref, bf16[512,2048]{1,0:T(8,128)(2,1)S(1)} %get-tuple-element.49.wb_ref.w_ref, bf16[1024,2048]{1,0:T(8,128)(2,1)S(1)} %get-tuple-element.51.wc_ref.w_ref, ...), custom_call_target="tpu_custom_call" | custom-call | flops 30000000 | bytes 1048576 | tf_op jit(solution)/shard_map/pallas_call | solution.py:266
  30.2 0.0 collective-permute-done.6.back_ref
  30.2 2.5 %shard_map.96 = (bf16[1024,2048]{1,0:T(8,128)(2,1)S(1)}, bf16[4,256,128]{2,1,0:T(8,128)(2,1)S(1)}, bf16[2,256,128]{2,1,0:T(8,128)(2,1)S(1)}, f32[3,256,128]{2,1,0:T(8,128)S(1)}) custom-call(f32[8,128]{1,0:T(8,128)S(1)} %get-tuple-element.46.gates_ref, bf16[1024,2048]{1,0:T(8,128)(2,1)S(1)} %get-tuple-element.51.wc_ref.w_ref, ...), custom_call_target="tpu_custom_call" | custom-call | flops 35000000 | bytes 1048576 | tf_op jit(solution)/shard_map/pallas_call | solution.py:266
  32.7 0.1 collective-permute-start.7
  32.8 1.0 %collective-permute-start.9 = (bf16[2,256,128]{2,1,0:T(8,128)(2,1)S(1)}, bf16[2,256,128]{2,1,0:T(8,128)(2,1)S(1)}, u32[]{:S(2)}, u32[]{:S(2)}) collective-permute-start(bf16[2,256,128]{2,1,0:T(8,128)(2,1)S(1)} %get-tuple-element.73), channel_id=1, source_target_pairs={{0,2},{1,3},{2,0},{3,1},{4,6},{5,7},{6,4},{7,5},{8,10},{9,11},{10,... | collective-permute-start | bytes 393224 | tf_op jit(solution)/shard_map/ppermute | solution.py:29
  33.8 1.3 %shard_map.95 = (bf16[512,2048]{1,0:T(8,128)(2,1)S(1)}, f32[2,256,128]{2,1,0:T(8,128)S(1)}) custom-call(bf16[512,2048]{1,0:T(8,128)(2,1)S(1)} %get-tuple-element.49.wb_ref.w_ref, bf16[128,2048]{1,0:T(8,128)(2,1)S(1)} %get-tuple-element.58.gt_ref, f32[8,256]{1,0:T(8,128)S(1)} %get-tuple-element.60.dot_ref, bf16[2048,128]{1,0:T(8,128)(2,1)S(1)} %get-tuple-element.62.qd_ref, ...), custom_call_target="tpu_custom_call" | custom-call | flops 17000000 | bytes 1048576 | tf_op jit(solution)/shard_map/pallas_call | solution.py:266
  35.1 0.0 collective-permute-done.7.back_ref.core_ref
  35.1 0.1 shard_map.97.order_ref
  35.1 1.2 %collective-permute-start.8 = (bf16[2,256,128]{2,1,0:T(8,128)(2,1)S(1)}, bf16[2,256,128]{2,1,0:T(8,128)(2,1)S(1)}, u32[]{:S(2)}, u32[]{:S(2)}) collective-permute-start(bf16[2,256,128]{2,1,0:T(8,128)(2,1)S(1)} %shard_map.97.order_ref), channel_id=1, source_target_pairs={{0,2},{1,3},{2,0},{3,1},{4,6},{5,7},{6,4},{7,5},{8,10},{9,11},{10,... | collective-permute-start | bytes 393224 | tf_op jit(solution)/shard_map/ppermute | solution.py:29
  36.3 1.3 %shard_map.98 = (bf16[512,2048]{1,0:T(8,128)(2,1)S(1)}, f32[2,256,128]{2,1,0:T(8,128)S(1)}) custom-call(bf16[512,2048]{1,0:T(8,128)(2,1)S(1)} %get-tuple-element.47.wa_ref.w_ref, bf16[128,2048]{1,0:T(8,128)(2,1)S(1)} %get-tuple-element.58.gt_ref, f32[8,256]{1,0:T(8,128)S(1)} %get-tuple-element.60.dot_ref, bf16[2048,128]{1,0:T(8,128)(2,1)S(1)} %get-tuple-element.61.qd_ref, ...), custom_call_target="tpu_custom_call" | custom-call | flops 17000000 | bytes 1048576 | tf_op jit(solution)/shard_map/pallas_call | solution.py:266
  37.6 1.6 %collective-permute-done.9.back_ref = bf16[2,256,128]{2,1,0:T(8,128)(2,1)S(1)} collective-permute-done((bf16[2,256,128]{2,1,0:T(8,128)(2,1)S(1)}, bf16[2,256,128]{2,1,0:T(8,128)(2,1)S(1)}, u32[]{:S(2)}, u32[]{:S(2)}) %collective-permute-start.9) | collective-permute-done | bytes 131104 | tf_op jit(solution)/shard_map/ppermute | solution.py:29
  39.2 3.9 %collective-permute-start.13 = (bf16[256,128]{1,0:T(8,128)(2,1)S(1)}, bf16[256,128]{1,0:T(8,128)(2,1)S(1)}, u32[]{:S(2)}, u32[]{:S(2)}) collective-permute-start(bf16[256,128]{1,0:T(8,128)(2,1)S(1)} %get-tuple-element.74.order_ref), channel_id=1, source_target_pairs={{1,249},{2,250},{3,251},{5,253},{6,254},{7,255},{9,1},{10,2},{11,3... | collective-permute-start | bytes 196616 | tf_op jit(solution)/shard_map/ppermute | solution.py:24
  43.1 11.7 %collective-permute-start.12 = (bf16[256,128]{1,0:T(8,128)(2,1)S(1)}, bf16[256,128]{1,0:T(8,128)(2,1)S(1)}, u32[]{:S(2)}, u32[]{:S(2)}) collective-permute-start(bf16[256,128]{1,0:T(8,128)(2,1)S(1)} %get-tuple-element.79), channel_id=1, source_target_pairs={{0,252},{1,253},{2,254},{3,255},{4,0},{5,1},{6,2},{7,3},{8,4},{9,5... | collective-permute-start | bytes 196616 | tf_op jit(solution)/shard_map/ppermute | solution.py:24
  54.7 0.0 collective-permute-done.8.chip_ref
  54.7 0.1 shard_map.100
  54.8 1.9 %collective-permute-start.11 = (bf16[256,128]{1,0:T(8,128)(2,1)S(1)}, bf16[256,128]{1,0:T(8,128)(2,1)S(1)}, u32[]{:S(2)}, u32[]{:S(2)}) collective-permute-start(bf16[256,128]{1,0:T(8,128)(2,1)S(1)} %get-tuple-element.75.order_ref), channel_id=1, source_target_pairs={{1,249},{2,250},{3,251},{5,253},{6,254},{7,255},{9,1},{10,2},{11,3... | collective-permute-start | bytes 196616 | tf_op jit(solution)/shard_map/ppermute | solution.py:24
  56.8 0.4 collective-permute-start.10
  57.2 0.0 collective-permute-done.13
  57.2 0.0 collective-permute-done.12
  57.2 0.7 %add_convert_fusion = bf16[256,128]{1,0:T(8,128)(2,1)} fusion(bf16[256,128]{1,0:T(8,128)(2,1)S(1)} %collective-permute-done.13, f32[256,128]{1,0:T(8,128)S(1)} %get-tuple-element.78, bf16[256,128]{1,0:T(8,128)(2,1)S(1)} %collective-permute-done.12), kind=kLoop, calls=%fused_computation.1 | loop fusion | flops 163840 | bytes 327680 | tf_op jit(solution)/shard_map/convert_element_type | solution.py:389
  57.9 2.3 %shard_map.101 = bf16[256,1024]{1,0:T(8,128)(2,1)} custom-call(bf16[512,2048]{1,0:T(8,128)(2,1)S(1)} %get-tuple-element.68.da_ref, bf16[512,2048]{1,0:T(8,128)(2,1)S(1)} %get-tuple-element.69.db_ref, bf16[1024,2048]{1,0:T(8,128)(2,1)S(1)} %get-tuple-element.70.dc_ref, f32[3,8,256]{2,1,0:T(8,128)S(1)} %get-tuple-element.57.coef_ref, ...), custom_call_target="tpu_custom_call" | custom-call | flops 30000000 | bytes 1048576 | tf_op jit(solution)/shard_map/pallas_call | solution.py:266
  60.2 2.3 %collective-permute-done.11 = bf16[256,128]{1,0:T(8,128)(2,1)S(1)} collective-permute-done((bf16[256,128]{1,0:T(8,128)(2,1)S(1)}, bf16[256,128]{1,0:T(8,128)(2,1)S(1)}, u32[]{:S(2)}, u32[]{:S(2)}) %collective-permute-start.11) | collective-permute-done | bytes 65568 | tf_op jit(solution)/shard_map/ppermute | solution.py:24
  62.5 0.0 collective-permute-done.10
  62.5 0.7 %add_convert_fusion.1 = bf16[256,128]{1,0:T(8,128)(2,1)} fusion(bf16[256,128]{1,0:T(8,128)(2,1)S(1)} %collective-permute-done.11, f32[256,128]{1,0:T(8,128)S(1)} %get-tuple-element.76, bf16[256,128]{1,0:T(8,128)(2,1)S(1)} %collective-permute-done.10), kind=kLoop, calls=%fused_computation.2 | loop fusion | flops 163840 | bytes 327680 | tf_op jit(solution)/shard_map/convert_element_type | solution.py:390
  (14 shorter events, 0.2 us)
Async XLA Ops:
  0.6 9.1 %copy-start.2 = (bf16[256,128]{1,0:T(8,128)(2,1)S(1)}, bf16[256,128]{1,0:T(8,128)(2,1)}, u32[]{:S(2)}) copy-start(bf16[256,128]{1,0:T(8,128)(2,1)} %v_ref.1) | copy-start | bytes 196612
  0.6 9.1 %copy-start.3 = (bf16[256,128]{1,0:T(8,128)(2,1)S(1)}, bf16[256,128]{1,0:T(8,128)(2,1)}, u32[]{:S(2)}) copy-start(bf16[256,128]{1,0:T(8,128)(2,1)} %k_ref.1) | copy-start | bytes 196612
  0.7 9.1 %copy-start = (bf16[256,1024]{1,0:T(8,128)(2,1)S(1)}, bf16[256,1024]{1,0:T(8,128)(2,1)}, u32[]{:S(2)}) copy-start(bf16[256,1024]{1,0:T(8,128)(2,1)} %q_ref.3) | copy-start | bytes 1572868
  0.7 9.1 %copy-start.1 = (bf16[256,1024]{1,0:T(8,128)(2,1)S(1)}, bf16[256,1024]{1,0:T(8,128)(2,1)}, u32[]{:S(2)}) copy-start(bf16[256,1024]{1,0:T(8,128)(2,1)} %g_ref.3) | copy-start | bytes 1572868
  1.7 8.5 %collective-permute-start = (bf16[2,256,128]{2,1,0:T(8,128)(2,1)S(1)}, bf16[2,256,128]{2,1,0:T(8,128)(2,1)S(1)}, u32[]{:S(2)}, u32[]{:S(2)}) collective-permute-start(bf16[2,256,128]{2,1,0:T(8,128)(2,1)S(1)} %pad_maximum_fusion), channel_id=1, source_target_pairs={{0,4},{1,5},{2,6},{3,7},{4,8},{5,9},{6,10},{7,11},{8,12},{9,13},{1... | collective-permute-start | bytes 393224 | tf_op jit(solution)/shard_map/ppermute | solution.py:24
  3.3 9.3 %collective-permute-start.1 = (bf16[2,256,128]{2,1,0:T(8,128)(2,1)S(1)}, bf16[2,256,128]{2,1,0:T(8,128)(2,1)S(1)}, u32[]{:S(2)}, u32[]{:S(2)}) collective-permute-start(bf16[2,256,128]{2,1,0:T(8,128)(2,1)S(1)} %pad_maximum_fusion), channel_id=1, source_target_pairs={{1,9},{2,10},{3,11},{5,13},{6,14},{7,15},{9,17},{10,18},{11,19},{1... | collective-permute-start | bytes 393224 | tf_op jit(solution)/shard_map/ppermute | solution.py:24
  8.2 0.7 %copy-start.4 = (s32[64]{0:T(128)S(1)}, s32[64]{0:T(128)}, u32[]{:S(2)}) copy-start(s32[64]{0:T(128)} %lengths_ref.1) | copy-start | bytes 772
  12.6 5.1 %collective-permute-start.2 = (bf16[2,256,128]{2,1,0:T(8,128)(2,1)S(1)}, bf16[2,256,128]{2,1,0:T(8,128)(2,1)S(1)}, u32[]{:S(2)}, u32[]{:S(2)}) collective-permute-start(bf16[2,256,128]{2,1,0:T(8,128)(2,1)S(1)} %shard_map.86.refs_2_), channel_id=1, source_target_pairs={{0,2},{1,3},{2,0},{3,1},{4,6},{5,7},{6,4},{7,5},{8,10},{9,11},{10,... | collective-permute-start | bytes 393224 | tf_op jit(solution)/shard_map/ppermute | solution.py:29
  17.7 1.8 %collective-permute-start.3 = (bf16[4,256,128]{2,1,0:T(8,128)(2,1)S(1)}, bf16[4,256,128]{2,1,0:T(8,128)(2,1)S(1)}, u32[]{:S(2)}, u32[]{:S(2)}) collective-permute-start(bf16[4,256,128]{2,1,0:T(8,128)(2,1)S(1)} %shard_map.88.refs_1_.refs_0_), channel_id=1, source_target_pairs={{0,1},{1,0},{2,3},{3,2},{4,5},{5,4},{6,7},{7,6},{8,9},{9,8},{10,11... | collective-permute-start | bytes 786440 | tf_op jit(solution)/shard_map/ppermute | solution.py:29
  17.9 6.0 %collective-permute-start.4 = (bf16[2,256,128]{2,1,0:T(8,128)(2,1)S(1)}, bf16[2,256,128]{2,1,0:T(8,128)(2,1)S(1)}, u32[]{:S(2)}, u32[]{:S(2)}) collective-permute-start(bf16[2,256,128]{2,1,0:T(8,128)(2,1)S(1)} %shard_map.90.refs_1_), channel_id=1, source_target_pairs={{0,2},{1,3},{2,0},{3,1},{4,6},{5,7},{6,4},{7,5},{8,10},{9,11},{10,... | collective-permute-start | bytes 393224 | tf_op jit(solution)/shard_map/ppermute | solution.py:29
  23.9 3.8 %collective-permute-start.5 = (bf16[4,256,128]{2,1,0:T(8,128)(2,1)S(1)}, bf16[4,256,128]{2,1,0:T(8,128)(2,1)S(1)}, u32[]{:S(2)}, u32[]{:S(2)}) collective-permute-start(bf16[4,256,128]{2,1,0:T(8,128)(2,1)S(1)} %shard_map.92.order_ref), channel_id=1, source_target_pairs={{0,1},{1,0},{2,3},{3,2},{4,5},{5,4},{6,7},{7,6},{8,9},{9,8},{10,11... | collective-permute-start | bytes 786440 | tf_op jit(solution)/shard_map/ppermute | solution.py:29
  27.1 3.0 %collective-permute-start.6 = (bf16[4,256,128]{2,1,0:T(8,128)(2,1)S(1)}, bf16[4,256,128]{2,1,0:T(8,128)(2,1)S(1)}, u32[]{:S(2)}, u32[]{:S(2)}) collective-permute-start(bf16[4,256,128]{2,1,0:T(8,128)(2,1)S(1)} %get-tuple-element.66), channel_id=1, source_target_pairs={{0,1},{1,0},{2,3},{3,2},{4,5},{5,4},{6,7},{7,6},{8,9},{9,8},{10,11... | collective-permute-start | bytes 786440 | tf_op jit(solution)/shard_map/ppermute | solution.py:29
  32.7 2.4 %collective-permute-start.7 = (bf16[4,256,128]{2,1,0:T(8,128)(2,1)S(1)}, bf16[4,256,128]{2,1,0:T(8,128)(2,1)S(1)}, u32[]{:S(2)}, u32[]{:S(2)}) collective-permute-start(bf16[4,256,128]{2,1,0:T(8,128)(2,1)S(1)} %get-tuple-element.67), channel_id=1, source_target_pairs={{0,1},{1,0},{2,3},{3,2},{4,5},{5,4},{6,7},{7,6},{8,9},{9,8},{10,11... | collective-permute-start | bytes 786440 | tf_op jit(solution)/shard_map/ppermute | solution.py:29
  32.8 6.4 %collective-permute-start.9 = (bf16[2,256,128]{2,1,0:T(8,128)(2,1)S(1)}, bf16[2,256,128]{2,1,0:T(8,128)(2,1)S(1)}, u32[]{:S(2)}, u32[]{:S(2)}) collective-permute-start(bf16[2,256,128]{2,1,0:T(8,128)(2,1)S(1)} %get-tuple-element.73), channel_id=1, source_target_pairs={{0,2},{1,3},{2,0},{3,1},{4,6},{5,7},{6,4},{7,5},{8,10},{9,11},{10,... | collective-permute-start | bytes 393224 | tf_op jit(solution)/shard_map/ppermute | solution.py:29
  35.1 19.6 %collective-permute-start.8 = (bf16[2,256,128]{2,1,0:T(8,128)(2,1)S(1)}, bf16[2,256,128]{2,1,0:T(8,128)(2,1)S(1)}, u32[]{:S(2)}, u32[]{:S(2)}) collective-permute-start(bf16[2,256,128]{2,1,0:T(8,128)(2,1)S(1)} %shard_map.97.order_ref), channel_id=1, source_target_pairs={{0,2},{1,3},{2,0},{3,1},{4,6},{5,7},{6,4},{7,5},{8,10},{9,11},{10,... | collective-permute-start | bytes 393224 | tf_op jit(solution)/shard_map/ppermute | solution.py:29
  39.2 18.0 %collective-permute-start.13 = (bf16[256,128]{1,0:T(8,128)(2,1)S(1)}, bf16[256,128]{1,0:T(8,128)(2,1)S(1)}, u32[]{:S(2)}, u32[]{:S(2)}) collective-permute-start(bf16[256,128]{1,0:T(8,128)(2,1)S(1)} %get-tuple-element.74.order_ref), channel_id=1, source_target_pairs={{1,249},{2,250},{3,251},{5,253},{6,254},{7,255},{9,1},{10,2},{11,3... | collective-permute-start | bytes 196616 | tf_op jit(solution)/shard_map/ppermute | solution.py:24
  43.1 14.2 %collective-permute-start.12 = (bf16[256,128]{1,0:T(8,128)(2,1)S(1)}, bf16[256,128]{1,0:T(8,128)(2,1)S(1)}, u32[]{:S(2)}, u32[]{:S(2)}) collective-permute-start(bf16[256,128]{1,0:T(8,128)(2,1)S(1)} %get-tuple-element.79), channel_id=1, source_target_pairs={{0,252},{1,253},{2,254},{3,255},{4,0},{5,1},{6,2},{7,3},{8,4},{9,5... | collective-permute-start | bytes 196616 | tf_op jit(solution)/shard_map/ppermute | solution.py:24
  54.8 7.7 %collective-permute-start.11 = (bf16[256,128]{1,0:T(8,128)(2,1)S(1)}, bf16[256,128]{1,0:T(8,128)(2,1)S(1)}, u32[]{:S(2)}, u32[]{:S(2)}) collective-permute-start(bf16[256,128]{1,0:T(8,128)(2,1)S(1)} %get-tuple-element.75.order_ref), channel_id=1, source_target_pairs={{1,249},{2,250},{3,251},{5,253},{6,254},{7,255},{9,1},{10,2},{11,3... | collective-permute-start | bytes 196616 | tf_op jit(solution)/shard_map/ppermute | solution.py:24
  56.8 5.7 %collective-permute-start.10 = (bf16[256,128]{1,0:T(8,128)(2,1)S(1)}, bf16[256,128]{1,0:T(8,128)(2,1)S(1)}, u32[]{:S(2)}, u32[]{:S(2)}) collective-permute-start(bf16[256,128]{1,0:T(8,128)(2,1)S(1)} %get-tuple-element.77), channel_id=1, source_target_pairs={{0,252},{1,253},{2,254},{3,255},{4,0},{5,1},{6,2},{7,3},{8,4},{9,5... | collective-permute-start | bytes 196616 | tf_op jit(solution)/shard_map/ppermute | solution.py:24
